TPU v7x, 128 devices: a whole 4x4x4 slice. The times are simulated.
128 devices in a mesh: user: 32 (over y, x, core), item: 4 (over z).
Axes of the slice: x: 4, y: 4, z: 4, core: 2. Of those that a mesh axis runs over, the one named last changes fastest.
Arguments:
- user_factors: float32 [16384, 256], P('user'), may hold values from -1.5 to 1.5
- item_factors: float32 [131072, 256], P(('user', 'item')), may hold values from -1.5 to 1.5
- feedback: bfloat16 [512, 16384, 128], P('item', 'user'), may hold values from 0 to 1
- item_pick: int32 [128, 128], replicated, may hold values from 0 to 7, as said below
- user_noise: float32 [16384, 256], P('user'), may hold values from -6 to 6
- item_noise: float32 [131072, 256], P(('user', 'item')), may hold values from -6 to 6
Outputs:
- new_user: float32 [16384, 256], P('user')
- new_item: float32 [131072, 256], P(('user', 'item'))
Inputs may be any that keep to these rules, and one draw needn't show every extreme that they name: For every owner o and every user slab u, the 4 entries item_pick[u * 4 + i, o] are distinct, so that no tile appears twice.
All inputs are finite; a program needn't handle non-finite values.
Results may differ from a plain program's by a relative error of at most 0.00058.
Values may be sent and summed in bfloat16 or wider, within the bound.
No kernel may reach another device: no remote copies, remote signals or barrier semaphores. Data moves between devices by JAX's collectives and lax.ppermute only.
A program may use at most 192 MiB of HBM per device.

v0:
```python
import math

import jax
import jax.numpy as jnp
from jax import lax
from jax.sharding import PartitionSpec as P

step_size = 0.01
item_step = 0.1
prior_weight = 1.0
noise_scale = math.sqrt(0.02)
item_noise_scale = math.sqrt(0.2)


def local(user_factors, item_factors, feedback, item_pick, user_noise, item_noise):
    devices = lax.axis_size(("user", "item"))
    own_index = lax.axis_index(("user", "item"))
    tile_size = feedback.shape[2]
    rank_width = item_factors.shape[1]
    held_blocks = item_factors.shape[0] // tile_size
    item_half = item_factors.astype(jnp.bfloat16).reshape(held_blocks, tile_size, rank_width)
    wanted = lax.dynamic_slice_in_dim(item_pick, own_index, 1, 1)[:, 0]
    outgoing = jnp.take(item_half, wanted, axis=0)
    arrived = lax.all_to_all(outgoing, ("user", "item"), split_axis=0, concat_axis=0, tiled=True)
    user_slab = user_factors.astype(jnp.bfloat16)
    scores = jnp.einsum("uk,ntk->nut", user_slab, arrived, preferred_element_type=jnp.float32)
    residual = (jax.nn.sigmoid(scores) - feedback.astype(jnp.float32)).astype(jnp.bfloat16)
    user_grad = jnp.einsum("nut,ntk->uk", residual, arrived, preferred_element_type=jnp.float32)
    item_part = jnp.einsum("nut,uk->ntk", residual, user_slab, preferred_element_type=jnp.float32)
    returned = lax.all_to_all(
        item_part, ("user", "item"), split_axis=0, concat_axis=0, tiled=True
    ).reshape(devices, tile_size * rank_width)
    selector = (wanted[None, :] == jnp.arange(held_blocks, dtype=jnp.int32)[:, None]).astype(
        jnp.float32
    )
    item_grad = jnp.dot(
        selector, returned, precision=lax.Precision.HIGHEST, preferred_element_type=jnp.float32
    ).reshape(item_factors.shape)
    new_item = (
        item_factors
        - item_step * (item_grad + prior_weight * item_factors)
        + item_noise_scale * item_noise
    )
    grad_total = lax.psum(user_grad, "item")
    new_user = (
        user_factors
        - step_size * (grad_total + prior_weight * user_factors)
        + noise_scale * user_noise
    )
    return (new_user, new_item)


def solution(mesh):
    in_specs = (
        P("user", None),
        P(("user", "item"), None),
        P("item", "user", None),
        P(),
        P("user", None),
        P(("user", "item"), None),
    )
    out_specs = (P("user", None), P(("user", "item"), None))
    return jax.shard_map(local, mesh=mesh, in_specs=in_specs, out_specs=out_specs, check_vma=False)
```

profile of v0, /device:TPU:10, one launch (start us, length us, event | category | flops | bytes accessed | tf_op | source)
XLA Modules:
  0.0 441.5 jit_solution(9927355187179912926)
XLA Ops:
  7.2 1.0 and_reduce_fusion
  8.2 1.5 dynamic-slice_reduce_fusion
  9.7 1.3 convert_element_type.13
  11.0 6.5 %gather_fusion = bf16[128,128,256]{2,1,0:T(8,128)(2,1)} fusion(bf16[8,128,256]{2,1,0:T(8,128)(2,1)S(1)} %bitcast.19, s32[1024]{0:T(1024)S(1)} %pad_clamp_fusion), kind=kCustom, calls=%fused_computation | custom fusion | bytes 16777728 | tf_op jit(solution)/shard_map/jit(_take)/gather | solution.py:23
  17.5 7.4 %broadcast_select_fusion = bf16[128,128,256]{2,1,0:T(8,128)(2,1)} fusion(bf16[128,128,256]{2,1,0:T(8,128)(2,1)} %gather_fusion, pred[128]{0:T(512)(128)(4,1)S(1)} %and_reduce_fusion), kind=kLoop, calls=%fused_computation.3 | loop fusion | flops 4194304 | bytes 16777344 | tf_op jit(solution)/shard_map/jit(_take)/select_n | solution.py:23
  25.0 10.9 %all-to-all-start = ((bf16[128,128,256]{2,1,0:T(8,128)(2,1)}), bf16[128,128,256]{2,1,0:T(8,128)(2,1)}, u32[]{:S(2)}, u32[]{:S(2)}) async-start(bf16[128,128,256]{2,1,0:T(8,128)(2,1)} %broadcast_select_fusion), calls=%async_computation | async-start | bytes 16777216 | tf_op jit(solution)/shard_map/all_to_all | solution.py:24
  35.8 0.0 copy-start.1
  35.9 22.5 %copy.10 = bf16[128,512,128]{1,2,0:T(8,128)(2,1)} copy(bf16[128,512,128]{2,1,0:T(8,128)(2,1)} %param.8) | data formatting | bytes 33554432 | tf_op args[2]
  58.4 77.1 %all-to-all-done = bf16[128,128,256]{2,1,0:T(8,128)(2,1)} async-done(((bf16[128,128,256]{2,1,0:T(8,128)(2,1)}), bf16[128,128,256]{2,1,0:T(8,128)(2,1)}, u32[]{:S(2)}, u32[]{:S(2)}) %all-to-all-start) | async-done | bytes 8388640 | tf_op jit(solution)/shard_map/all_to_all | solution.py:24
  135.5 0.0 copy-done.1
  135.5 18.8 %fusion = bf16[128,512,128]{1,2,0:T(8,128)(2,1)} fusion(bf16[128,512,128]{1,2,0:T(8,128)(2,1)} %copy.10, bf16[128,128,256]{2,1,0:T(8,128)(2,1)} %all-to-all-done, f32[512,256]{1,0:T(8,128)S(1)} %copy-done.1), kind=kOutput, calls=%fused_computation.2 | convolution fusion | flops 4345430016 | bytes 42467328 | tf_op jit(solution)/shard_map/uk,ntk->nut/dot_general | solution.py:26
  154.2 16.0 %fusion.1 = f32[128,128,256]{2,1,0:T(8,128)} fusion(bf16[128,512,128]{1,2,0:T(8,128)(2,1)} %fusion, f32[512,256]{1,0:T(8,128)S(1)} %copy-done.1), kind=kOutput, calls=%fused_computation.7 | convolution fusion | flops 4295098368 | bytes 34078720 | tf_op jit(solution)/shard_map/nut,uk->ntk/dot_general | solution.py:29
  170.2 11.7 %all-to-all-start.1 = ((f32[128,128,256]{2,1,0:T(8,128)}), f32[128,128,256]{2,1,0:T(8,128)}, u32[]{:S(2)}, u32[]{:S(2)}) async-start(f32[128,128,256]{2,1,0:T(8,128)} %fusion.1), calls=%async_computation.1 | async-start | bytes 33554432 | tf_op jit(solution)/shard_map/all_to_all | solution.py:30
  182.0 0.0 copy-start.2
  182.0 0.2 all-reduce.2.cloned.1.call-start
  182.2 13.5 %convolution_bitcast_fusion = f32[512,256]{1,0:T(8,128)} fusion(bf16[128,512,128]{1,2,0:T(8,128)(2,1)} %fusion, bf16[128,128,256]{2,1,0:T(8,128)(2,1)} %all-to-all-done), kind=kOutput, calls=%fused_computation.4 | convolution fusion | flops 4294967296 | bytes 25690112 | tf_op jit(solution)/shard_map/nut,ntk->uk/dot_general | solution.py:28
  195.7 0.0 all-reduce.2.cloned.1.call-update
  195.7 202.4 %all-reduce.2.cloned.1.call-done = f32[512,256]{1,0:T(8,128)} async-done(((f32[512,256]{1,0:T(8,128)}), f32[512,256]{1,0:T(8,128)}) %all-reduce.2.cloned.1.call-update) | async-done | bytes 524304 | tf_op jit(solution)/shard_map/psum | solution.py:44
  398.1 0.0 copy-done.2
  398.1 1.9 multiply_add_fusion.1
  400.1 10.9 %all-to-all-done.1 = f32[128,128,256]{2,1,0:T(8,128)} async-done(((f32[128,128,256]{2,1,0:T(8,128)}), f32[128,128,256]{2,1,0:T(8,128)}, u32[]{:S(2)}, u32[]{:S(2)}) %all-to-all-start.1) | async-done | bytes 16777248 | tf_op jit(solution)/shard_map/all_to_all | solution.py:30
  411.0 0.0 copy-start.3
  411.0 15.5 %copy.13 = f32[16,8,128,256]{3,1,2,0:T(8,128)S(1)} copy(f32[16,8,128,256]{3,2,1,0:T(8,128)} %bitcast.4) | data formatting | bytes 33554432
  426.5 0.0 copy-start
  426.5 0.0 copy-done.3
  426.5 5.6 %fusion.7 = f32[8,32768]{1,0:T(8,128)S(1)} fusion(f32[128,32768]{1,0:T(8,128)S(1)} %bitcast.20, s32[128]{0:T(128)S(1)} %copy-done.3), kind=kOutput, calls=%fused_computation.18 | convolution fusion | flops 402654208 | bytes 17826304 | tf_op jit(solution)/shard_map/dot_general | solution.py:36
  432.0 0.2 reshape.20
  432.2 0.0 copy-done
  432.2 2.4 multiply_add_fusion
  (1 shorter events, 0.0 us)
Async XLA Ops:
  25.0 110.5 %all-to-all-start = ((bf16[128,128,256]{2,1,0:T(8,128)(2,1)}), bf16[128,128,256]{2,1,0:T(8,128)(2,1)}, u32[]{:S(2)}, u32[]{:S(2)}) async-start(bf16[128,128,256]{2,1,0:T(8,128)(2,1)} %broadcast_select_fusion), calls=%async_computation | async-start | bytes 16777216 | tf_op jit(solution)/shard_map/all_to_all | solution.py:24
  35.8 99.6 %copy-start.1 = (f32[512,256]{1,0:T(8,128)S(1)}, f32[512,256]{1,0:T(8,128)}, u32[]{:S(2)}) copy-start(f32[512,256]{1,0:T(8,128)} %param.6) | copy-start | bytes 1572868
  170.2 240.7 %all-to-all-start.1 = ((f32[128,128,256]{2,1,0:T(8,128)}), f32[128,128,256]{2,1,0:T(8,128)}, u32[]{:S(2)}, u32[]{:S(2)}) async-start(f32[128,128,256]{2,1,0:T(8,128)} %fusion.1), calls=%async_computation.1 | async-start | bytes 33554432 | tf_op jit(solution)/shard_map/all_to_all | solution.py:30
  182.0 216.1 %copy-start.2 = (f32[512,256]{1,0:T(8,128)S(1)}, f32[512,256]{1,0:T(8,128)}, u32[]{:S(2)}) copy-start(f32[512,256]{1,0:T(8,128)} %param.10) | copy-start | bytes 1572868
  182.0 216.1 %all-reduce.2.cloned.1.call-start = ((), (), s32[]{:S(2)}) async-start(), calls=%async_computation.2 | async-start | bytes 1048576 | tf_op jit(solution)/shard_map/psum | solution.py:44
  411.0 15.5 %copy-start.3 = (s32[128]{0:T(128)S(1)}, s32[128]{0:T(128)}, u32[]{:S(2)}) copy-start(s32[128]{0:T(128)} %get-tuple-element.2) | copy-start | bytes 1540
  426.5 5.7 %copy-start = (f32[1024,256]{1,0:T(8,128)S(1)}, f32[1024,256]{1,0:T(8,128)}, u32[]{:S(2)}) copy-start(f32[1024,256]{1,0:T(8,128)} %param.7) | copy-start | bytes 3145732
Sparse Core Ops, SparseCore 0:
  195.8 202.2 all-reduce.1
where the time goes:
time: 442 us; the launch traced here: 441 us
  waiting for transfers between devices  290 us (66%)
  matrix products  53.8 us (12%)
  local copies, waits for them, and re-layouts  44.7 us (10%)
  starting transfers between devices  22.8 us (5%)
  other arithmetic  15.6 us (4%)
  between operations  14.1 us (3%)
    psum x1, waiting for transfers between devices, local(): grad_total = lax.psum(user_grad, 'item')  202 us
    all_to_all x1, waiting for transfers between devices, local(): lax.all_to_all(outgoing, ('user', 'item'), split_axis=0, concat_axis=0, t...  77.1 us
    unnamed x10, local copies, waits for them, and re-layouts  38 us
    dot_general x1, matrix products, local(): jnp.einsum('uk,ntk->nut', user_slab, arrived, preferred_element_type=jnp....  18.8 us
    dot_general x1, matrix products, local(): jnp.einsum('nut,uk->ntk', residual, user_slab, preferred_element_type=jnp...  16 us
    dot_general x1, matrix products, local(): jnp.einsum('nut,ntk->uk', residual, arrived, preferred_element_type=jnp.f...  13.5 us
    all_to_all x1, starting transfers between devices, local(): lax.all_to_all(item_part, ('user', 'item'), split_axis=0, concat_axis=0,...  11.7 us
    all_to_all x1, waiting for transfers between devices, local(): lax.all_to_all(item_part, ('user', 'item'), split_axis=0, concat_axis=0,...  10.9 us
  transfers between devices with their start and end apart: 3, of which 3 were waited for; matrix products, arithmetic and copies ran while one was open for 9% of the time, Pallas kernels for 0%

commit v1 on v0

v1 whole, which is shorter than its diff:
```python
import functools
import math

import jax
import jax.numpy as jnp
from jax import lax
from jax.experimental import pallas as pl
from jax.experimental.pallas import tpu as pltpu
from jax.sharding import PartitionSpec as P

step_size = 0.01
item_step = 0.1
prior_weight = 1.0
noise_scale = math.sqrt(0.02)
item_noise_scale = math.sqrt(0.2)

PARTS = 2
VMEM_LIMIT = 60 * 1024 * 1024
AXES = ("user", "item")

CODE_FLOOR = 2.0**-20
CODE_RATE = 32700.0 / math.log2(1.0 + 776.0 / CODE_FLOOR)


def encode(part):
    level = jnp.log2(1.0 + jnp.abs(part) * (1.0 / CODE_FLOOR)) * CODE_RATE + 0.5
    level = level.astype(jnp.int32)
    return jnp.where(part < 0.0, -level, level).astype(jnp.int16)


def decode(code):
    code = code.astype(jnp.float32)
    size = jnp.exp2(jnp.abs(code) * (1.0 / CODE_RATE)) * CODE_FLOOR - CODE_FLOOR
    return jnp.where(code < 0.0, -size, size)


def pack_kernel(per_step, rows, wanted_ref, seg_ref, item_ref, out_ref):
    step = pl.program_id(0)
    start = pl.multiple_of(seg_ref[0] * rows, rows)
    for j in range(per_step):
        block = wanted_ref[step * per_step + j]
        out_ref[j] = item_ref[block, pl.ds(start, rows), :].astype(jnp.bfloat16)


def pack(item_blocks, wanted, seg, rows):
    held, tile, rank = item_blocks.shape
    count = wanted.shape[0]
    per_step = 16
    return pl.pallas_call(
        functools.partial(pack_kernel, per_step, rows),
        out_shape=jax.ShapeDtypeStruct((count, rows, rank), jnp.bfloat16),
        grid_spec=pltpu.PrefetchScalarGridSpec(
            num_scalar_prefetch=2,
            grid=(count // per_step,),
            in_specs=[pl.BlockSpec((held, tile, rank), lambda g, *_: (0, 0, 0))],
            out_specs=pl.BlockSpec((per_step, rows, rank), lambda g, *_: (g, 0, 0)),
        ),
        cost_estimate=pl.CostEstimate(
            flops=0, bytes_accessed=count * rows * rank * 2, transcendentals=0
        ),
        compiler_params=pltpu.CompilerParams(vmem_limit_bytes=VMEM_LIMIT),
    )(wanted, seg, item_blocks)


def tile_kernel(chunk, groups, user_ref, arrived_ref, feedback_ref, grad_ref, code_ref):
    @pl.when(pl.program_id(0) == 0)
    def _():
        grad_ref[...] = jnp.zeros_like(grad_ref)

    user = user_ref[...]
    users = user.shape[0]
    rows = arrived_ref.shape[1]
    tile = feedback_ref.shape[2]
    lane = lax.broadcasted_iota(jnp.int32, (users, tile), 1)
    residuals, blocks = [], []
    for pair in range(groups // 2):
        sides, items = [], []
        for half in range(2):
            first = (pair * 2 + half) * PARTS
            order = [first + (s - chunk) % PARTS for s in range(PARTS)]
            items += [arrived_ref[o] for o in order]
            seen = feedback_ref[order[PARTS - 1]].astype(jnp.float32)
            for s in range(PARTS - 2, -1, -1):
                seen = jnp.where(
                    lane < (s + 1) * rows, feedback_ref[order[s]].astype(jnp.float32), seen
                )
            sides.append(seen)
        block = jnp.concatenate(items, axis=0)
        scores = lax.dot_general(
            user, block, (((1,), (1,)), ((), ())), preferred_element_type=jnp.float32
        )
        residual = jnp.concatenate(
            [
                (jnp.tanh(scores[:, h * tile : (h + 1) * tile] * 0.5) * 0.5 + 0.5 - sides[h]).astype(
                    jnp.bfloat16
                )
                for h in range(2)
            ],
            axis=1,
        )
        part = lax.dot_general(
            residual, user, (((0,), (0,)), ((), ())), preferred_element_type=jnp.float32
        )
        code = encode(part)
        for half in range(2):
            first = (pair * 2 + half) * PARTS
            for s in range(PARTS):
                at = half * tile + s * rows
                code_ref[first + (s - chunk) % PARTS] = code[at : at + rows]
        residuals.append(residual)
        blocks.append(block)
    grad_ref[...] += jnp.dot(
        jnp.concatenate(residuals, axis=1),
        jnp.concatenate(blocks, axis=0),
        preferred_element_type=jnp.float32,
    )


def tiles(chunk, user_half, arrived, feedback):
    count, rows, rank = arrived.shape
    users = user_half.shape[0]
    tile = feedback.shape[2]
    per_step = 8
    work = count * rows * users * rank * 6
    return pl.pallas_call(
        functools.partial(tile_kernel, chunk, per_step // PARTS),
        out_shape=(
            jax.ShapeDtypeStruct((users, rank), jnp.float32),
            jax.ShapeDtypeStruct((count, rows, rank), jnp.int16),
        ),
        grid=(count // per_step,),
        in_specs=[
            pl.BlockSpec((users, rank), lambda g: (0, 0)),
            pl.BlockSpec((per_step, rows, rank), lambda g: (g, 0, 0)),
            pl.BlockSpec((per_step, users, tile), lambda g: (g, 0, 0)),
        ],
        out_specs=(
            pl.BlockSpec((users, rank), lambda g: (0, 0)),
            pl.BlockSpec((per_step, rows, rank), lambda g: (g, 0, 0)),
        ),
        cost_estimate=pl.CostEstimate(
            flops=work, bytes_accessed=count * users * tile * 2, transcendentals=0
        ),
        compiler_params=pltpu.CompilerParams(vmem_limit_bytes=VMEM_LIMIT),
    )(user_half, arrived, feedback)


def settle_kernel(
    per_step, last, wanted_ref, seg_ref, code_ref, item_ref, noise_ref, *refs
):
    if last:
        _, gathered_ref, user_ref, user_noise_ref, out_ref, new_user_ref, sum_ref = refs
        user = user_ref[...]
        total = gathered_ref[0]
        for z in range(1, gathered_ref.shape[0]):
            total = total + gathered_ref[z]
        new_user_ref[...] = (
            user - step_size * (total + prior_weight * user)
        ) + noise_scale * user_noise_ref[...]
    else:
        *_, out_ref, sum_ref = refs
    step = pl.program_id(0)

    @pl.when(step == 0)
    def _():
        sum_ref[...] = jnp.zeros_like(sum_ref)

    for j in range(per_step):
        block = wanted_ref[step * per_step + j]
        sum_ref[block] += decode(code_ref[j])

    @pl.when(step == pl.num_programs(0) - 1)
    def _():
        item = item_ref[...]
        out_ref[...] = (
            item - item_step * (sum_ref[...] + prior_weight * item)
        ) + item_noise_scale * noise_ref[...]


def settle(wanted, seg, codes, item_blocks, noise_blocks, before, user_side):
    count, rows, rank = codes.shape
    held = item_blocks.shape[0]
    per_step = 16
    steps = count // per_step
    part = pl.BlockSpec((held, rows, rank), lambda g, wanted_ref, seg_ref: (0, seg_ref[0], 0))
    in_specs = [pl.BlockSpec((per_step, rows, rank), lambda g, *_: (g, 0, 0)), part, part]
    out_specs = [part]
    out_shape = [jax.ShapeDtypeStruct(item_blocks.shape, jnp.float32)]
    operands = [wanted, seg, codes, item_blocks, noise_blocks]
    aliases = {}
    if before is not None:
        in_specs.append(pl.BlockSpec(memory_space=pl.ANY))
        aliases[len(operands)] = 0
        operands.append(before)
    if user_side is not None:
        users = user_side[1].shape[0]
        share = pl.BlockSpec((users // steps, rank), lambda g, *_: (g, 0))
        in_specs += [
            pl.BlockSpec((user_side[0].shape[0], users // steps, rank), lambda g, *_: (0, g, 0)),
            share,
            share,
        ]
        operands += user_side
        out_specs.append(share)
        out_shape.append(jax.ShapeDtypeStruct((users, rank), jnp.float32))
    return pl.pallas_call(
        functools.partial(settle_kernel, per_step, user_side is not None),
        out_shape=out_shape,
        grid_spec=pltpu.PrefetchScalarGridSpec(
            num_scalar_prefetch=2,
            grid=(steps,),
            in_specs=in_specs,
            out_specs=out_specs,
            scratch_shapes=[pltpu.VMEM((held, rows, rank), jnp.float32)],
        ),
        input_output_aliases=aliases,
        cost_estimate=pl.CostEstimate(
            flops=0, bytes_accessed=count * rows * rank * 8, transcendentals=0
        ),
        compiler_params=pltpu.CompilerParams(vmem_limit_bytes=VMEM_LIMIT),
    )(*operands)


def local(user_factors, item_factors, feedback, item_pick, user_noise, item_noise):
    own_index = lax.axis_index(AXES)
    tile_size = feedback.shape[2]
    rank_width = item_factors.shape[1]
    held_blocks = item_factors.shape[0] // tile_size
    rows = tile_size // PARTS
    wanted = lax.dynamic_slice_in_dim(item_pick, own_index, 1, 1)[:, 0]
    item_blocks = item_factors.reshape(held_blocks, tile_size, rank_width)
    noise_blocks = item_noise.reshape(held_blocks, tile_size, rank_width)
    user_half = user_factors.astype(jnp.bfloat16)
    segs = [((chunk + own_index) % PARTS).astype(jnp.int32)[None] for chunk in range(PARTS)]
    arrived = [
        lax.all_to_all(
            pack(item_blocks, wanted, seg, rows), AXES, split_axis=0, concat_axis=0, tiled=True
        )
        for seg in segs
    ]
    grads, returned = [], []
    for chunk in range(PARTS):
        grad, codes = tiles(chunk, user_half, arrived[chunk], feedback)
        grads.append(grad)
        returned.append(lax.all_to_all(codes, AXES, split_axis=0, concat_axis=0, tiled=True))
    gathered = lax.all_gather(functools.reduce(jnp.add, grads), "item")
    new_item = None
    for chunk in range(PARTS):
        user_side = [gathered, user_factors, user_noise] if chunk == PARTS - 1 else None
        new_item, *new_user = settle(
            wanted, segs[chunk], returned[chunk], item_blocks, noise_blocks, new_item, user_side
        )
    return (new_user[0], new_item.reshape(item_factors.shape))


def solution(mesh):
    in_specs = (
        P("user", None),
        P(("user", "item"), None),
        P("item", "user", None),
        P(),
        P("user", None),
        P(("user", "item"), None),
    )
    out_specs = (P("user", None), P(("user", "item"), None))
    return jax.shard_map(local, mesh=mesh, in_specs=in_specs, out_specs=out_specs, check_vma=False)
```

time: 442 us -> 282 us (0.64)
  waiting for transfers between devices: 290 us -> 161 us
  Pallas kernels: 0 us -> 71.4 us
  matrix products: 53.8 us -> 0 us
  local copies, waits for them, and re-layouts: 44.7 us -> 1.52 us
  other arithmetic: 15.6 us -> 1.59 us
  starting transfers between devices: 22.8 us -> 29.4 us
    psum x1 -> x0, waiting for transfers between devices: 202 us -> none  [local(): grad_total = lax.psum(user_grad, 'item')]
    pallas_call x0 -> x6, Pallas kernels: none -> 71.4 us  [the longest x2 43 us: tiles(): pl.pallas_call(functools.partial(tile_kernel, chunk, per_step // PARTS),...]
    all_gather x0 -> x1, waiting for transfers between devices: none -> 56.4 us  [local(): gathered = lax.all_gather(functools.reduce(jnp.add, grads), 'item')]
    dot_general x4 -> x0, matrix products: 53.8 us -> none  [the longest x1 18.8 us: local(): jnp.einsum('uk,ntk->nut', user_slab, arrived, preferred_element_type=jnp....]
    unnamed x10 -> x8, local copies, waits for them, and re-layouts: 38 us -> 0.84 us
    all_to_all x2 -> x4, waiting for transfers between devices: 88 us -> 104 us  [the longest x2 74.5 us: local(): lax.all_to_all(pack(item_blocks, wanted, seg, rows), AXES, split_axis=0,...]
    select_n x1 -> x0, other arithmetic: 7.41 us -> none  [local(): outgoing = jnp.take(item_half, wanted, axis=0)]
    all_to_all x2 -> x4, starting transfers between devices: 22.6 us -> 29.4 us  [the longest x2 17 us: local(): lax.all_to_all(pack(item_blocks, wanted, seg, rows), AXES, split_axis=0,...]
  transfers between devices with their start and end apart: 3 -> 5, of which waited for: 3 -> 4; matrix products, arithmetic and copies ran while one was open for 9% -> 1% of each run, Pallas kernels for 0% -> 20%
where the time goes in v1:
time: 282 us; the launch traced here: 279 us
  waiting for transfers between devices  161 us (57%)
  Pallas kernels  71.4 us (25%)
  starting transfers between devices  29.4 us (10%)
  between operations  14.1 us (5%)
    all_to_all x2, waiting for transfers between devices, local(): lax.all_to_all(pack(item_blocks, wanted, seg, rows), AXES, split_axis=0,...  74.5 us
    all_gather x1, waiting for transfers between devices, local(): gathered = lax.all_gather(functools.reduce(jnp.add, grads), 'item')  56.4 us
    pallas_call x2, Pallas kernels, tiles(): pl.pallas_call(functools.partial(tile_kernel, chunk, per_step // PARTS),...  43 us
    all_to_all x2, waiting for transfers between devices, local(): lax.all_to_all(codes, AXES, split_axis=0, concat_axis=0, tiled=True)  29.7 us
    pallas_call x2, Pallas kernels, settle(): pl.pallas_call(functools.partial(settle_kernel, per_step, user_side is no...  17.2 us
    all_to_all x2, starting transfers between devices, local(): lax.all_to_all(pack(item_blocks, wanted, seg, rows), AXES, split_axis=0,...  17 us
    all_to_all x2, starting transfers between devices, local(): lax.all_to_all(codes, AXES, split_axis=0, concat_axis=0, tiled=True)  12.4 us
    pallas_call x2, Pallas kernels, pack(): pl.pallas_call(functools.partial(pack_kernel, per_step, rows), out_shape=...  11.2 us
  transfers between devices with their start and end apart: 5, of which 4 were waited for; matrix products, arithmetic and copies ran while one was open for 1% of the time, Pallas kernels for 20%

profile of v1, /device:TPU:10, one launch (start us, length us, event | category | flops | bytes accessed | tf_op | source)
XLA Modules:
  0.0 278.6 jit_solution(4517356089396910258)
XLA Ops:
  7.2 0.0 copy-start
  7.2 0.8 copy-done
  8.0 0.7 dynamic-slice_reduce_fusion.wanted_ref
  8.7 5.6 %shard_map.79 = bf16[128,64,256]{2,1,0:T(8,128)(2,1)} custom-call(s32[128]{0:T(128)} %dynamic-slice_reduce_fusion.wanted_ref, s32[1]{0:T(128)} %bitcast.3.seg_ref, f32[8,128,256]{2,1,0:T(8,128)} %bitcast.6), custom_call_target="tpu_custom_call" | custom-call | bytes 4194304 | tf_op jit(solution)/shard_map/pallas_call | solution.py:49
  14.3 10.9 %all-to-all-start.2 = ((bf16[128,64,256]{2,1,0:T(8,128)(2,1)}), bf16[128,64,256]{2,1,0:T(8,128)(2,1)}, u32[]{:S(2)}, u32[]{:S(2)}) async-start(bf16[128,64,256]{2,1,0:T(8,128)(2,1)} %shard_map.79), calls=%async_computation.2 | async-start | bytes 8388608 | tf_op jit(solution)/shard_map/all_to_all | solution.py:236
  25.2 5.6 %shard_map.77 = bf16[128,64,256]{2,1,0:T(8,128)(2,1)} custom-call(s32[128]{0:T(128)} %dynamic-slice_reduce_fusion.wanted_ref, s32[1]{0:T(128)} %bitcast.seg_ref, f32[8,128,256]{2,1,0:T(8,128)} %bitcast.7), custom_call_target="tpu_custom_call" | custom-call | bytes 4194304 | tf_op jit(solution)/shard_map/pallas_call | solution.py:49
  30.7 0.0 copy-start.1
  30.8 45.5 %all-to-all-done.2.arrived_ref = bf16[128,64,256]{2,1,0:T(8,128)(2,1)} async-done(((bf16[128,64,256]{2,1,0:T(8,128)(2,1)}), bf16[128,64,256]{2,1,0:T(8,128)(2,1)}, u32[]{:S(2)}, u32[]{:S(2)}) %all-to-all-start.2) | async-done | bytes 4194336 | tf_op jit(solution)/shard_map/all_to_all | solution.py:236
  76.3 6.1 %all-to-all-start = ((bf16[128,64,256]{2,1,0:T(8,128)(2,1)}), bf16[128,64,256]{2,1,0:T(8,128)(2,1)}, u32[]{:S(2)}, u32[]{:S(2)}) async-start(bf16[128,64,256]{2,1,0:T(8,128)(2,1)} %shard_map.77), calls=%async_computation | async-start | bytes 8388608 | tf_op jit(solution)/shard_map/all_to_all | solution.py:236
  82.4 0.0 copy-done.1
  82.4 0.7 convert_element_type.3.user_ref
  83.2 21.5 %shard_map.80 = (f32[512,256]{1,0:T(8,128)}, s16[128,64,256]{2,1,0:T(8,128)(2,1)}) custom-call(bf16[512,256]{1,0:T(8,128)(2,1)} %convert_element_type.3.user_ref, bf16[128,64,256]{2,1,0:T(8,128)(2,1)} %all-to-all-done.2.arrived_ref, bf16[128,512,128]{2,1,0:T(8,128)(2,1)} %feedback_ref.3), custom_call_target="tpu_custom_call" | custom-call | flops 6442450944 | bytes 16777216 | tf_op jit(solution)/shard_map/pallas_call | solution.py:125
  104.7 29.0 %all-to-all-done.arrived_ref = bf16[128,64,256]{2,1,0:T(8,128)(2,1)} async-done(((bf16[128,64,256]{2,1,0:T(8,128)(2,1)}), bf16[128,64,256]{2,1,0:T(8,128)(2,1)}, u32[]{:S(2)}, u32[]{:S(2)}) %all-to-all-start) | async-done | bytes 4194336 | tf_op jit(solution)/shard_map/all_to_all | solution.py:236
  133.6 6.1 %all-to-all-start.3 = ((s16[128,64,256]{2,1,0:T(8,128)(2,1)}), s16[128,64,256]{2,1,0:T(8,128)(2,1)}, u32[]{:S(2)}, u32[]{:S(2)}) async-start(s16[128,64,256]{2,1,0:T(8,128)(2,1)} %get-tuple-element.9), calls=%async_computation.3 | async-start | bytes 8388608 | tf_op jit(solution)/shard_map/all_to_all | solution.py:245
  139.8 21.5 %shard_map.78 = (f32[512,256]{1,0:T(8,128)}, s16[128,64,256]{2,1,0:T(8,128)(2,1)}) custom-call(bf16[512,256]{1,0:T(8,128)(2,1)} %convert_element_type.3.user_ref, bf16[128,64,256]{2,1,0:T(8,128)(2,1)} %all-to-all-done.arrived_ref, bf16[128,512,128]{2,1,0:T(8,128)(2,1)} %feedback_ref.3), custom_call_target="tpu_custom_call" | custom-call | flops 6442450944 | bytes 16777216 | tf_op jit(solution)/shard_map/pallas_call | solution.py:125
  161.3 29.7 %all-to-all-done.3.code_ref = s16[128,64,256]{2,1,0:T(8,128)(2,1)} async-done(((s16[128,64,256]{2,1,0:T(8,128)(2,1)}), s16[128,64,256]{2,1,0:T(8,128)(2,1)}, u32[]{:S(2)}, u32[]{:S(2)}) %all-to-all-start.3) | async-done | bytes 4194336 | tf_op jit(solution)/shard_map/all_to_all | solution.py:245
  191.0 0.0 copy-start.2
  191.0 0.0 copy-start.3
  191.0 6.3 %all-to-all-start.1 = ((s16[128,64,256]{2,1,0:T(8,128)(2,1)}), s16[128,64,256]{2,1,0:T(8,128)(2,1)}, u32[]{:S(2)}, u32[]{:S(2)}) async-start(s16[128,64,256]{2,1,0:T(8,128)(2,1)} %get-tuple-element.8), calls=%async_computation.1 | async-start | bytes 8388608 | tf_op jit(solution)/shard_map/all_to_all | solution.py:245
  197.2 0.0 all-gather.3.cloned.1.call-start
  197.3 0.0 copy-done.2
  197.3 0.0 copy-done.3
  197.3 0.9 add.24
  198.2 0.0 all-gather.3.cloned.1.call-update
  198.2 8.2 %shard_map.81.refs_0_ = f32[8,128,256]{2,1,0:T(8,128)} custom-call(s32[128]{0:T(128)} %dynamic-slice_reduce_fusion.wanted_ref, s32[1]{0:T(128)} %bitcast.3.seg_ref, s16[128,64,256]{2,1,0:T(8,128)(2,1)} %all-to-all-done.3.code_ref, f32[8,128,256]{2,1,0:T(8,128)} %bitcast.8, f32[8,128,256]{2,1,0:T(8,128)} %bitcast.10), custom_call_target="tpu_custom_call" | custom-call | bytes 16777216 | tf_op jit(solution)/shard_map/pallas_call | solution.py:206
  206.4 56.4 %all-gather.3.cloned.1.call-done = f32[2048,256]{1,0:T(8,128)} async-done(((f32[512,256]{1,0:T(8,128)}), f32[2048,256]{1,0:T(8,128)}) %all-gather.3.cloned.1.call-update) | async-done | bytes 2097168 | tf_op jit(solution)/shard_map/all_gather | solution.py:246
  262.8 0.0 all-to-all-done.1.code_ref
  262.8 9.0 %shard_map.82 = (f32[8,128,256]{2,1,0:T(8,128)}, f32[512,256]{1,0:T(8,128)}) custom-call(s32[128]{0:T(128)} %dynamic-slice_reduce_fusion.wanted_ref, s32[1]{0:T(128)} %bitcast.seg_ref, s16[128,64,256]{2,1,0:T(8,128)(2,1)} %all-to-all-done.1.code_ref, f32[8,128,256]{2,1,0:T(8,128)} %bitcast.9, ...), custom_call_target="tpu_custom_call", output_to_operand_aliasing={{0}: (5, {})} | custom-call | bytes 16777216 | tf_op jit(solution)/shard_map/pallas_call | solution.py:206
Async XLA Ops:
  7.2 0.8 copy-start
  14.3 62.0 %all-to-all-start.2 = ((bf16[128,64,256]{2,1,0:T(8,128)(2,1)}), bf16[128,64,256]{2,1,0:T(8,128)(2,1)}, u32[]{:S(2)}, u32[]{:S(2)}) async-start(bf16[128,64,256]{2,1,0:T(8,128)(2,1)} %shard_map.79), calls=%async_computation.2 | async-start | bytes 8388608 | tf_op jit(solution)/shard_map/all_to_all | solution.py:236
  30.7 51.7 %copy-start.1 = (f32[512,256]{1,0:T(8,128)S(1)}, f32[512,256]{1,0:T(8,128)}, u32[]{:S(2)}) copy-start(f32[512,256]{1,0:T(8,128)} %refs_2_.1) | copy-start | bytes 1572868
  76.3 57.3 %all-to-all-start = ((bf16[128,64,256]{2,1,0:T(8,128)(2,1)}), bf16[128,64,256]{2,1,0:T(8,128)(2,1)}, u32[]{:S(2)}, u32[]{:S(2)}) async-start(bf16[128,64,256]{2,1,0:T(8,128)(2,1)} %shard_map.77), calls=%async_computation | async-start | bytes 8388608 | tf_op jit(solution)/shard_map/all_to_all | solution.py:236
  133.6 57.3 %all-to-all-start.3 = ((s16[128,64,256]{2,1,0:T(8,128)(2,1)}), s16[128,64,256]{2,1,0:T(8,128)(2,1)}, u32[]{:S(2)}, u32[]{:S(2)}) async-start(s16[128,64,256]{2,1,0:T(8,128)(2,1)} %get-tuple-element.9), calls=%async_computation.3 | async-start | bytes 8388608 | tf_op jit(solution)/shard_map/all_to_all | solution.py:245
  191.0 6.3 %copy-start.2 = (f32[512,256]{1,0:T(8,128)S(1)}, f32[512,256]{1,0:T(8,128)}, u32[]{:S(2)}) copy-start(f32[512,256]{1,0:T(8,128)} %get-tuple-element.10) | copy-start | bytes 1572868
  191.0 6.3 %copy-start.3 = (f32[512,256]{1,0:T(8,128)S(1)}, f32[512,256]{1,0:T(8,128)}, u32[]{:S(2)}) copy-start(f32[512,256]{1,0:T(8,128)} %get-tuple-element.11) | copy-start | bytes 1572868
  191.0 71.8 %all-to-all-start.1 = ((s16[128,64,256]{2,1,0:T(8,128)(2,1)}), s16[128,64,256]{2,1,0:T(8,128)(2,1)}, u32[]{:S(2)}, u32[]{:S(2)}) async-start(s16[128,64,256]{2,1,0:T(8,128)(2,1)} %get-tuple-element.8), calls=%async_computation.1 | async-start | bytes 8388608 | tf_op jit(solution)/shard_map/all_to_all | solution.py:245
  197.2 65.5 %all-gather.3.cloned.1.call-start = ((), (), s32[]{:S(2)}) async-start(), calls=%async_computation.4 | async-start | bytes 2621440 | tf_op jit(solution)/shard_map/all_gather | solution.py:246
Sparse Core Ops, SparseCore 0:
  200.3 62.4 all-gather.2

commit v2 on v0

v2 whole, which is shorter than its diff:
```python
import functools
import math

import jax
import jax.numpy as jnp
from jax import lax
from jax.experimental import pallas as pl
from jax.experimental.pallas import tpu as pltpu
from jax.sharding import Mesh
from jax.sharding import PartitionSpec as P

step_size = 0.01
item_step = 0.1
prior_weight = 1.0
noise_scale = math.sqrt(0.02)
item_noise_scale = math.sqrt(0.2)

VMEM_LIMIT = 63 * 1024 * 1024
SETTLE_COST = 1024
AXES = ("y", "x", "c", "z")
SIZES = (4, 4, 2, 4)

CODE_FLOOR = 2.0**-20
ITEM_RATE = 32700.0 / math.log(1.0 + 776.0 / CODE_FLOOR)
USER_RATE = 32700.0 / math.log(1.0 + 24800.0 / CODE_FLOOR)


def encode(part, rate):
    level = jnp.log(1.0 + jnp.abs(part) * (1.0 / CODE_FLOOR)) * rate + 0.5
    level = level.astype(jnp.int32)
    return jnp.where(part < 0.0, -level, level).astype(jnp.int16)


def decode(code, rate):
    code = code.astype(jnp.float32)
    size = jnp.exp(jnp.abs(code) * (1.0 / rate)) * CODE_FLOOR - CODE_FLOOR
    return jnp.where(code < 0.0, -size, size)


def place_of(own):
    return own // 32, own // 8 % 4, own // 4 % 2, own % 4


def call(kernel, scalars, operands, grid, in_specs, out_specs, out_shape, work, moved, scratch=(), aliases={}):
    return pl.pallas_call(
        kernel,
        out_shape=out_shape,
        grid_spec=pltpu.PrefetchScalarGridSpec(
            num_scalar_prefetch=len(scalars),
            grid=grid,
            in_specs=in_specs,
            out_specs=out_specs,
            scratch_shapes=scratch,
        ),
        input_output_aliases=aliases,
        cost_estimate=pl.CostEstimate(flops=work, bytes_accessed=moved, transcendentals=0),
        compiler_params=pltpu.CompilerParams(vmem_limit_bytes=VMEM_LIMIT),
    )(*scalars, *operands)


def whole(shape):
    return pl.BlockSpec(shape, lambda g, *_: (0,) * len(shape))


def along(shape):
    return pl.BlockSpec(shape, lambda g, *_: (g,) + (0,) * (len(shape) - 1))


ANY = pl.BlockSpec(memory_space=pl.ANY)


SEGMENTS = 4


def segments_of(p, first):
    return [(p + 1 + k) % SEGMENTS for k in range(SEGMENTS - 1)] if first else [p]


def row_slice(segment, rows):
    return pl.ds(pl.multiple_of(segment * rows, rows), rows)


def pack_kernel(first, own_ref, pick_ref, item_ref, out_ref, half_ref, sem):
    own = own_ref[0]
    count = out_ref.shape[0]
    rows = item_ref.shape[1] // SEGMENTS
    for k, segment in enumerate(segments_of(place_of(own)[3], first)):
        half_ref[:, k * rows : (k + 1) * rows, :] = item_ref[:, row_slice(segment, rows), :].astype(
            jnp.bfloat16
        )

    def send(e, _):
        pltpu.make_async_copy(half_ref.at[pick_ref[e, own]], out_ref.at[e], sem).start()
        return 0

    lax.fori_loop(0, count, send, 0, unroll=8)
    pltpu.make_async_copy(out_ref, out_ref, sem).wait()


def pack(first, own, item_pick, item_blocks):
    held, tile, rank = item_blocks.shape
    count = item_pick.shape[0]
    rows = tile // SEGMENTS * (SEGMENTS - 1 if first else 1)
    return call(
        functools.partial(pack_kernel, first),
        (own, item_pick),
        (item_blocks,),
        (1,),
        [whole(item_blocks.shape)],
        ANY,
        jax.ShapeDtypeStruct((count, rows, rank), jnp.bfloat16),
        0,
        count * rows * rank * 2,
        [pltpu.VMEM((held, rows, rank), jnp.bfloat16), pltpu.SemaphoreType.DMA],
    )


def work_on(first, user, arrived_ref, feedback_ref, code_ref):
    users, tile = feedback_ref.shape[1:]
    rows = tile // SEGMENTS
    lane = lax.broadcasted_iota(jnp.int32, (users, tile), 1)
    tiles = []
    for group in range(0, feedback_ref.shape[0], SEGMENTS):
        seen = [feedback_ref[group + p].astype(jnp.float32) for p in range(SEGMENTS)]
        for k in range(SEGMENTS - 1 if first else 1):
            sources = [(s - 1 - k) % SEGMENTS if first else s for s in range(SEGMENTS)]
            mixed = seen[sources[SEGMENTS - 1]]
            for s in range(SEGMENTS - 2, -1, -1):
                mixed = jnp.where(lane < (s + 1) * rows, seen[sources[s]], mixed)
            tiles.append((mixed, [group + p for p in sources], slice(k * rows, (k + 1) * rows)))
    residuals, blocks = [], []
    for pair in range(0, len(tiles), 2):
        both = tiles[pair : pair + 2]
        block = jnp.concatenate([arrived_ref[o, at] for _, owners, at in both for o in owners], axis=0)
        scores = lax.dot_general(
            user, block, (((1,), (1,)), ((), ())), preferred_element_type=jnp.float32
        )
        sides = []
        for h, (mixed, _, _) in enumerate(both):
            chance = jnp.tanh(scores[:, h * tile : (h + 1) * tile] * 0.5) * 0.5 + 0.5
            sides.append((chance - mixed).astype(jnp.bfloat16))
        residual = jnp.concatenate(sides, axis=1)
        part = lax.dot_general(
            residual, user, (((0,), (0,)), ((), ())), preferred_element_type=jnp.float32
        )
        code = encode(part, ITEM_RATE)
        for h, (_, owners, at) in enumerate(both):
            for s, o in enumerate(owners):
                code_ref[o, at] = code[h * tile + s * rows : h * tile + (s + 1) * rows]
        residuals.append(residual)
        blocks.append(block)
    return jnp.dot(
        jnp.concatenate(residuals, axis=1),
        jnp.concatenate(blocks, axis=0),
        preferred_element_type=jnp.float32,
    )


def first_kernel(user_ref, arrived_ref, feedback_ref, grad_ref, code_ref):
    @pl.when(pl.program_id(0) == 0)
    def _():
        grad_ref[...] = jnp.zeros_like(grad_ref)

    grad_ref[...] += work_on(True, user_ref[...], arrived_ref, feedback_ref, code_ref)


def last_kernel(user_ref, arrived_ref, feedback_ref, before_ref, grad_code_ref, code_ref, grad_ref):
    @pl.when(pl.program_id(0) == 0)
    def _():
        grad_ref[...] = before_ref[...]

    grad_ref[...] += work_on(False, user_ref[...], arrived_ref, feedback_ref, code_ref)

    @pl.when(pl.program_id(0) == pl.num_programs(0) - 1)
    def _():
        grad_code_ref[...] = encode(grad_ref[...], USER_RATE)


def tiles_of(user_half, arrived, feedback, before=None):
    count, rows, rank = arrived.shape
    users, tile = feedback.shape[1:]
    last = before is not None
    per_step = 16 if last else 8
    return call(
        last_kernel if last else first_kernel,
        (),
        (user_half, arrived, feedback) + ((before,) if last else ()),
        (count // per_step,),
        [whole((users, rank)), along((per_step, rows, rank)), along((per_step, users, tile))]
        + [whole((users, rank))] * last,
        [whole((users, rank)), along((per_step, rows, rank))],
        [
            jax.ShapeDtypeStruct((users, rank), jnp.int16 if last else jnp.float32),
            jax.ShapeDtypeStruct((count, rows, rank), jnp.int16),
        ],
        count * rows * users * rank * 6,
        count * users * tile * 2,
        [pltpu.VMEM((users, rank), jnp.float32)] * last,
    )


def add_codes(wanted_ref, code_ref, sum_ref):
    step = pl.program_id(0)

    @pl.when(step == 0)
    def _():
        sum_ref[...] = jnp.zeros_like(sum_ref)

    per_step = code_ref.shape[0]
    for j in range(per_step):
        sum_ref[wanted_ref[step * per_step + j]] += decode(code_ref[j], ITEM_RATE)


def stepped(item, grad, noise):
    return (item - item_step * (grad + prior_weight * item)) + item_noise_scale * noise


def first_settle_kernel(z_ref, wanted_ref, code_ref, item_ref, noise_ref, out_ref, sum_ref):
    add_codes(wanted_ref, code_ref, sum_ref)

    @pl.when(pl.program_id(0) == pl.num_programs(0) - 1)
    def _():
        rows = item_ref.shape[1] // SEGMENTS
        for k, segment in enumerate(segments_of(z_ref[0], True)):
            at = row_slice(segment, rows)
            grad = sum_ref[:, k * rows : (k + 1) * rows, :]
            out_ref[:, at, :] = stepped(item_ref[:, at, :], grad, noise_ref[:, at, :])


def first_settle(z, wanted, codes, item_blocks, noise_blocks):
    count, rows, rank = codes.shape
    per_step = 16
    block = whole(item_blocks.shape)
    return call(
        first_settle_kernel,
        (z, wanted),
        (codes, item_blocks, noise_blocks),
        (count // per_step,),
        [along((per_step, rows, rank)), block, block],
        block,
        jax.ShapeDtypeStruct(item_blocks.shape, jnp.float32),
        0,
        SETTLE_COST,
        [pltpu.VMEM((item_blocks.shape[0], rows, rank), jnp.float32)],
    )


def last_settle_kernel(z_ref, wanted_ref, code_ref, item_ref, noise_ref, before_ref, out_ref, sum_ref):
    add_codes(wanted_ref, code_ref, sum_ref)

    @pl.when(pl.program_id(0) == pl.num_programs(0) - 1)
    def _():
        out_ref[...] = stepped(item_ref[...], sum_ref[...], noise_ref[...])


def last_settle(z, wanted, codes, item_blocks, noise_blocks, before):
    count, rows, rank = codes.shape
    held = item_blocks.shape[0]
    per_step = 32
    part = pl.BlockSpec((held, rows, rank), lambda g, z_ref, wanted_ref: (0, z_ref[0], 0))
    return call(
        last_settle_kernel,
        (z, wanted),
        (codes, item_blocks, noise_blocks, before),
        (count // per_step,),
        [along((per_step, rows, rank)), part, part, ANY],
        part,
        jax.ShapeDtypeStruct(item_blocks.shape, jnp.float32),
        0,
        count * rows * rank * 8,
        [pltpu.VMEM((held, rows, rank), jnp.float32)],
        {5: 0},
    )


def user_kernel(z_ref, *refs):
    *code_refs, user_ref, noise_ref, out_ref, grads_ref = refs
    for j in range(4):
        grads_ref[(z_ref[0] + 4 - j) % 4] = decode(code_refs[j][...], USER_RATE)
    total = grads_ref[0] + grads_ref[1] + grads_ref[2] + grads_ref[3]
    user = user_ref[...]
    out_ref[...] = (user - step_size * (total + prior_weight * user)) + noise_scale * noise_ref[...]


def step_users(z, codes, user_factors, user_noise):
    users, rank = user_factors.shape
    steps = 4
    share = along((users // steps, rank))
    return call(
        user_kernel,
        (z,),
        (*codes, user_factors, user_noise),
        (steps,),
        [share] * 6,
        share,
        jax.ShapeDtypeStruct((users, rank), jnp.float32),
        0,
        users * rank * 16,
        [pltpu.VMEM((4, users // steps, rank), jnp.float32)],
    )


def shift(array, axis, j):
    return array if j == 0 else lax.ppermute(array, axis, [(i, (i + j) % 4) for i in range(4)])


def local(user_factors, item_factors, feedback, item_pick, user_noise, item_noise):
    own_index = lax.axis_index(AXES).astype(jnp.int32)
    own = own_index[None]
    z = lax.axis_index("z").astype(jnp.int32)[None]
    tile_size = feedback.shape[2]
    rank_width = item_factors.shape[1]
    held_blocks = item_factors.shape[0] // tile_size
    item_blocks = item_factors.reshape(held_blocks, tile_size, rank_width)
    noise_blocks = item_noise.reshape(held_blocks, tile_size, rank_width)
    user_half = user_factors.astype(jnp.bfloat16)
    to_all = functools.partial(
        lax.all_to_all, axis_name=AXES, split_axis=0, concat_axis=0, tiled=True
    )

    arrived = [to_all(pack(first, own, item_pick, item_blocks)) for first in (True, False)]
    picks, _ = lax.optimization_barrier((item_pick, arrived[0]))
    wanted = lax.dynamic_slice_in_dim(picks, own_index, 1, 1)[:, 0]
    grad, codes = tiles_of(user_half, arrived[0], feedback)
    returned = to_all(codes)
    grad_code, last_codes = tiles_of(user_half, arrived[1], feedback, grad)
    last_returned = to_all(last_codes)
    grad_codes = [shift(grad_code, "z", j) for j in range(4)]
    new_item = first_settle(z, wanted, returned, item_blocks, noise_blocks)
    new_item = last_settle(z, wanted, last_returned, item_blocks, noise_blocks, new_item)
    new_item, *grad_codes = lax.optimization_barrier((new_item, *grad_codes))
    new_user = step_users(z, grad_codes, user_factors, user_noise)
    return (new_user, new_item.reshape(item_factors.shape))


def solution(mesh):
    grid = Mesh(mesh.devices.reshape(SIZES), AXES)
    users, items = AXES[:3], AXES
    in_specs = (
        P(users, None),
        P(items, None),
        P("z", users, None),
        P(),
        P(users, None),
        P(items, None),
    )
    out_specs = (P(users, None), P(items, None))
    return jax.shard_map(local, mesh=grid, in_specs=in_specs, out_specs=out_specs, check_vma=False)
```

time: 442 us -> 263 us (0.60)
  waiting for transfers between devices: 290 us -> 151 us
  Pallas kernels: 0 us -> 67.7 us
  matrix products: 53.8 us -> 0 us
  local copies, waits for them, and re-layouts: 44.7 us -> 2.11 us
  other arithmetic: 15.6 us -> 0.73 us
  starting transfers between devices: 22.8 us -> 37.1 us
  between operations: 14.1 us -> 0.73 us
    psum x1 -> x0, waiting for transfers between devices: 202 us -> none  [local(): grad_total = lax.psum(user_grad, 'item')]
    pallas_call x0 -> x7, Pallas kernels: none -> 67.7 us  [call(): pl.pallas_call(kernel, out_shape=out_shape, grid_spec=pltpu.PrefetchScala...]
    all_to_all x2 -> x4, waiting for transfers between devices: 88 us -> 148 us  [the longest x2 75 us: local(): to_all(pack(first, own, item_pick, item_blocks))]
    dot_general x4 -> x0, matrix products: 53.8 us -> none  [the longest x1 18.8 us: local(): jnp.einsum('uk,ntk->nut', user_slab, arrived, preferred_element_type=jnp....]
    unnamed x10, local copies, waits for them, and re-layouts: 38 us -> 1.42 us
    all_to_all x2 -> x4, starting transfers between devices: 22.6 us -> 31 us  [the longest x2 17.6 us: local(): to_all(pack(first, own, item_pick, item_blocks))]
    select_n x1 -> x0, other arithmetic: 7.41 us -> none  [local(): outgoing = jnp.take(item_half, wanted, axis=0)]
    gather x1 -> x0, local copies, waits for them, and re-layouts: 6.53 us -> none  [local(): outgoing = jnp.take(item_half, wanted, axis=0)]
  transfers between devices with their start and end apart: 3 -> 7, of which waited for: 3 -> 5; matrix products, arithmetic and copies ran while one was open for 9% -> 1% of each run, Pallas kernels for 0% -> 22%
where the time goes in v2:
time: 263 us; the launch traced here: 260 us
  waiting for transfers between devices  151 us (57%)
  Pallas kernels  67.7 us (26%)
  starting transfers between devices  37.1 us (14%)
    all_to_all x2, waiting for transfers between devices, local(): to_all(pack(first, own, item_pick, item_blocks))  75 us
    pallas_call x7, Pallas kernels, call(): pl.pallas_call(kernel, out_shape=out_shape, grid_spec=pltpu.PrefetchScala...  67.7 us
    all_to_all x1, waiting for transfers between devices, local(): returned = to_all(codes)  61.2 us
    all_to_all x2, starting transfers between devices, local(): to_all(pack(first, own, item_pick, item_blocks))  17.6 us
    all_to_all x1, waiting for transfers between devices, local(): last_returned = to_all(last_codes)  11.5 us
    all_to_all x1, starting transfers between devices, local(): last_returned = to_all(last_codes)  6.81 us
    all_to_all x1, starting transfers between devices, local(): returned = to_all(codes)  6.55 us
    ppermute x3, starting transfers between devices, shift(): lax.ppermute(array, axis, [(i, (i + j) % 4) for i in range(4)])  6.14 us
  transfers between devices with their start and end apart: 7, of which 5 were waited for; matrix products, arithmetic and copies ran while one was open for 1% of the time, Pallas kernels for 22%

profile of v2, /device:TPU:10, one launch (start us, length us, event | category | flops | bytes accessed | tf_op | source)
XLA Modules:
  0.0 259.6 jit_solution(7605384302249605810)
XLA Ops:
  0.6 5.7 %shard_map.77 = bf16[128,96,256]{2,1,0:T(8,128)(2,1)} custom-call(s32[1]{0:T(128)} %bitcast.1.own_ref, s32[128,128]{1,0:T(8,128)} %pick_ref.3, f32[8,128,256]{2,1,0:T(8,128)} %bitcast.5), custom_call_target="tpu_custom_call" | custom-call | bytes 6291456 | tf_op jit(solution)/shard_map/pallas_call | solution.py:45
  6.3 10.8 %all-to-all-start = ((bf16[128,96,256]{2,1,0:T(8,128)(2,1)}), bf16[128,96,256]{2,1,0:T(8,128)(2,1)}, u32[]{:S(2)}, u32[]{:S(2)}) async-start(bf16[128,96,256]{2,1,0:T(8,128)(2,1)} %shard_map.77), calls=%async_computation | async-start | bytes 12582912 | tf_op jit(solution)/shard_map/all_to_all | solution.py:321
  17.1 0.0 copy-start
  17.1 4.4 %shard_map.78 = bf16[128,32,256]{2,1,0:T(8,128)(2,1)} custom-call(s32[1]{0:T(128)} %bitcast.1.own_ref, s32[128,128]{1,0:T(8,128)} %pick_ref.3, f32[8,128,256]{2,1,0:T(8,128)} %bitcast.6), custom_call_target="tpu_custom_call" | custom-call | bytes 2097152 | tf_op jit(solution)/shard_map/pallas_call | solution.py:45
  21.6 71.1 %all-to-all-done.arrived_ref = bf16[128,96,256]{2,1,0:T(8,128)(2,1)} async-done(((bf16[128,96,256]{2,1,0:T(8,128)(2,1)}), bf16[128,96,256]{2,1,0:T(8,128)(2,1)}, u32[]{:S(2)}, u32[]{:S(2)}) %all-to-all-start) | async-done | bytes 6291488 | tf_op jit(solution)/shard_map/all_to_all | solution.py:321
  92.6 6.8 %all-to-all-start.1 = ((bf16[128,32,256]{2,1,0:T(8,128)(2,1)}), bf16[128,32,256]{2,1,0:T(8,128)(2,1)}, u32[]{:S(2)}, u32[]{:S(2)}) async-start(bf16[128,32,256]{2,1,0:T(8,128)(2,1)} %shard_map.78), calls=%async_computation.1 | async-start | bytes 4194304 | tf_op jit(solution)/shard_map/all_to_all | solution.py:321
  99.4 0.0 copy-done
  99.5 0.7 convert_element_type.3.user_ref
  100.2 24.0 %shard_map.79 = (f32[512,256]{1,0:T(8,128)}, s16[128,96,256]{2,1,0:T(8,128)(2,1)}) custom-call(bf16[512,256]{1,0:T(8,128)(2,1)} %convert_element_type.3.user_ref, bf16[128,96,256]{2,1,0:T(8,128)(2,1)} %all-to-all-done.arrived_ref, bf16[128,512,128]{2,1,0:T(8,128)(2,1)} %feedback_ref.3), custom_call_target="tpu_custom_call" | custom-call | flops 9663676416 | bytes 16777216 | tf_op jit(solution)/shard_map/pallas_call | solution.py:45
  124.1 3.9 %all-to-all-done.1.arrived_ref = bf16[128,32,256]{2,1,0:T(8,128)(2,1)} async-done(((bf16[128,32,256]{2,1,0:T(8,128)(2,1)}), bf16[128,32,256]{2,1,0:T(8,128)(2,1)}, u32[]{:S(2)}, u32[]{:S(2)}) %all-to-all-start.1) | async-done | bytes 2097184 | tf_op jit(solution)/shard_map/all_to_all | solution.py:321
  128.0 6.6 %all-to-all-start.3 = ((s16[128,96,256]{2,1,0:T(8,128)(2,1)}), s16[128,96,256]{2,1,0:T(8,128)(2,1)}, u32[]{:S(2)}, u32[]{:S(2)}) async-start(s16[128,96,256]{2,1,0:T(8,128)(2,1)} %get-tuple-element.15), calls=%async_computation.3 | async-start | bytes 12582912 | tf_op jit(solution)/shard_map/all_to_all | solution.py:325
  134.6 0.0 copy-start.1
  134.6 14.3 %shard_map.80 = (s16[512,256]{1,0:T(8,128)(2,1)}, s16[128,32,256]{2,1,0:T(8,128)(2,1)}) custom-call(bf16[512,256]{1,0:T(8,128)(2,1)} %convert_element_type.3.user_ref, bf16[128,32,256]{2,1,0:T(8,128)(2,1)} %all-to-all-done.1.arrived_ref, bf16[128,512,128]{2,1,0:T(8,128)(2,1)} %feedback_ref.3, f32[512,256]{1,0:T(8,128)} %get-tuple-element.13.before_ref), custom_call_target="tpu_custom_call" | custom-call | flops 3221225472 | bytes 16777216 | tf_op jit(solution)/shard_map/pallas_call | solution.py:45
  148.9 61.2 %all-to-all-done.3.code_ref = s16[128,96,256]{2,1,0:T(8,128)(2,1)} async-done(((s16[128,96,256]{2,1,0:T(8,128)(2,1)}), s16[128,96,256]{2,1,0:T(8,128)(2,1)}, u32[]{:S(2)}, u32[]{:S(2)}) %all-to-all-start.3) | async-done | bytes 6291488 | tf_op jit(solution)/shard_map/all_to_all | solution.py:325
  210.2 6.8 %all-to-all-start.2 = ((s16[128,32,256]{2,1,0:T(8,128)(2,1)}), s16[128,32,256]{2,1,0:T(8,128)(2,1)}, u32[]{:S(2)}, u32[]{:S(2)}) async-start(s16[128,32,256]{2,1,0:T(8,128)(2,1)} %get-tuple-element.14), calls=%async_computation.2 | async-start | bytes 4194304 | tf_op jit(solution)/shard_map/all_to_all | solution.py:327
  217.0 1.7 collective-permute-start
  218.7 3.2 %collective-permute-start.1 = (s16[512,256]{1,0:T(8,128)(2,1)}, s16[512,256]{1,0:T(8,128)(2,1)S(1)}, u32[]{:S(2)}, u32[]{:S(2)}) collective-permute-start(s16[512,256]{1,0:T(8,128)(2,1)} %get-tuple-element.17.refs_0_), channel_id=1, source_target_pairs={{0,2},{1,3},{2,0},{3,1},{4,6},{5,7},{6,4},{7,5},{8,10},{9,11},{10,... | collective-permute-start | bytes 786440 | tf_op jit(solution)/shard_map/ppermute | solution.py:304
  221.9 1.2 collective-permute-start.2
  223.1 0.0 copy-done.1
  223.1 0.7 dynamic-slice_reduce_fusion.wanted_ref
  223.8 10.3 %shard_map.81.before_ref = f32[8,128,256]{2,1,0:T(8,128)} custom-call(s32[1]{0:T(128)} %bitcast.z_ref, s32[128]{0:T(128)} %dynamic-slice_reduce_fusion.wanted_ref, s16[128,96,256]{2,1,0:T(8,128)(2,1)} %all-to-all-done.3.code_ref, f32[8,128,256]{2,1,0:T(8,128)} %bitcast.7, f32[8,128,256]{2,1,0:T(8,128)} %bitcast.9), custom_call_target="tpu_custom_call" | custom-call | bytes 1024 | tf_op jit(solution)/shard_map/pallas_call | solution.py:45
  234.2 11.5 %all-to-all-done.2.code_ref = s16[128,32,256]{2,1,0:T(8,128)(2,1)} async-done(((s16[128,32,256]{2,1,0:T(8,128)(2,1)}), s16[128,32,256]{2,1,0:T(8,128)(2,1)}, u32[]{:S(2)}, u32[]{:S(2)}) %all-to-all-start.2) | async-done | bytes 2097184 | tf_op jit(solution)/shard_map/all_to_all | solution.py:327
  245.7 5.0 %shard_map.82 = f32[8,128,256]{2,1,0:T(8,128)} custom-call(s32[1]{0:T(128)} %bitcast.z_ref, s32[128]{0:T(128)} %dynamic-slice_reduce_fusion.wanted_ref, s16[128,32,256]{2,1,0:T(8,128)(2,1)} %all-to-all-done.2.code_ref, f32[8,128,256]{2,1,0:T(8,128)} %bitcast.8, f32[8,128,256]{2,1,0:T(8,128)} %bitcast.10, ...), custom_call_target="tpu_custom_call", output_to_operand_aliasing={{}: (5, {})} | custom-call | bytes 8388608 | tf_op jit(solution)/shard_map/pallas_call | solution.py:45
  250.7 0.0 collective-permute-done.refs_1_
  250.7 0.0 copy-start.2
  250.7 3.5 %collective-permute-done.1.refs_2_ = s16[512,256]{1,0:T(8,128)(2,1)S(1)} collective-permute-done((s16[512,256]{1,0:T(8,128)(2,1)}, s16[512,256]{1,0:T(8,128)(2,1)S(1)}, u32[]{:S(2)}, u32[]{:S(2)}) %collective-permute-start.1) | collective-permute-done | bytes 262176 | tf_op jit(solution)/shard_map/ppermute | solution.py:304
  254.2 0.0 copy-start.3
  254.2 0.0 collective-permute-done.2.refs_3_
  254.2 0.0 copy-done.2
  254.2 0.7 copy-done.3
  254.9 0.0 copy-start.4
  254.9 0.7 copy-done.4
  255.6 4.0 %shard_map.83 = f32[512,256]{1,0:T(8,128)} custom-call(s32[1]{0:T(128)} %bitcast.z_ref, s16[512,256]{1,0:T(8,128)(2,1)} %get-tuple-element.17.refs_0_, s16[512,256]{1,0:T(8,128)(2,1)} %copy-done.2, s16[512,256]{1,0:T(8,128)(2,1)} %copy-done.3, s16[512,256]{1,0:T(8,128)(2,1)} %copy-done.4, f32[512,256]{1,0:T(8,128)} %refs_4_.1, f32[512,256]{1,0:T(8,128)} %refs_5_.1), custom_call_target="tpu_custom_call" | custom-call | bytes 2097152 | tf_op jit(solution)/shard_map/pallas_call | solution.py:45
Async XLA Ops:
  6.3 86.3 %all-to-all-start = ((bf16[128,96,256]{2,1,0:T(8,128)(2,1)}), bf16[128,96,256]{2,1,0:T(8,128)(2,1)}, u32[]{:S(2)}, u32[]{:S(2)}) async-start(bf16[128,96,256]{2,1,0:T(8,128)(2,1)} %shard_map.77), calls=%async_computation | async-start | bytes 12582912 | tf_op jit(solution)/shard_map/all_to_all | solution.py:321
  17.1 82.3 %copy-start = (f32[512,256]{1,0:T(8,128)S(1)}, f32[512,256]{1,0:T(8,128)}, u32[]{:S(2)}) copy-start(f32[512,256]{1,0:T(8,128)} %refs_4_.1) | copy-start | bytes 1572868
  92.6 35.4 %all-to-all-start.1 = ((bf16[128,32,256]{2,1,0:T(8,128)(2,1)}), bf16[128,32,256]{2,1,0:T(8,128)(2,1)}, u32[]{:S(2)}, u32[]{:S(2)}) async-start(bf16[128,32,256]{2,1,0:T(8,128)(2,1)} %shard_map.78), calls=%async_computation.1 | async-start | bytes 4194304 | tf_op jit(solution)/shard_map/all_to_all | solution.py:321
  128.0 82.1 %all-to-all-start.3 = ((s16[128,96,256]{2,1,0:T(8,128)(2,1)}), s16[128,96,256]{2,1,0:T(8,128)(2,1)}, u32[]{:S(2)}, u32[]{:S(2)}) async-start(s16[128,96,256]{2,1,0:T(8,128)(2,1)} %get-tuple-element.15), calls=%async_computation.3 | async-start | bytes 12582912 | tf_op jit(solution)/shard_map/all_to_all | solution.py:325
  134.6 88.5 %copy-start.1 = (s32[128,128]{1,0:T(8,128)S(1)}, s32[128,128]{1,0:T(8,128)}, u32[]{:S(2)}) copy-start(s32[128,128]{1,0:T(8,128)} %pick_ref.3) | copy-start | bytes 196612
  210.2 35.5 %all-to-all-start.2 = ((s16[128,32,256]{2,1,0:T(8,128)(2,1)}), s16[128,32,256]{2,1,0:T(8,128)(2,1)}, u32[]{:S(2)}, u32[]{:S(2)}) async-start(s16[128,32,256]{2,1,0:T(8,128)(2,1)} %get-tuple-element.14), calls=%async_computation.2 | async-start | bytes 4194304 | tf_op jit(solution)/shard_map/all_to_all | solution.py:327
  217.0 33.7 %collective-permute-start = (s16[512,256]{1,0:T(8,128)(2,1)}, s16[512,256]{1,0:T(8,128)(2,1)S(1)}, u32[]{:S(2)}, u32[]{:S(2)}) collective-permute-start(s16[512,256]{1,0:T(8,128)(2,1)} %get-tuple-element.17.refs_0_), channel_id=1, source_target_pairs={{0,1},{1,2},{2,3},{3,0},{4,5},{5,6},{6,7},{7,4},{8,9},{9,10},{10,1... | collective-permute-start | bytes 786440 | tf_op jit(solution)/shard_map/ppermute | solution.py:304
  218.7 35.5 %collective-permute-start.1 = (s16[512,256]{1,0:T(8,128)(2,1)}, s16[512,256]{1,0:T(8,128)(2,1)S(1)}, u32[]{:S(2)}, u32[]{:S(2)}) collective-permute-start(s16[512,256]{1,0:T(8,128)(2,1)} %get-tuple-element.17.refs_0_), channel_id=1, source_target_pairs={{0,2},{1,3},{2,0},{3,1},{4,6},{5,7},{6,4},{7,5},{8,10},{9,11},{10,... | collective-permute-start | bytes 786440 | tf_op jit(solution)/shard_map/ppermute | solution.py:304
  221.9 32.3 %collective-permute-start.2 = (s16[512,256]{1,0:T(8,128)(2,1)}, s16[512,256]{1,0:T(8,128)(2,1)S(1)}, u32[]{:S(2)}, u32[]{:S(2)}) collective-permute-start(s16[512,256]{1,0:T(8,128)(2,1)} %get-tuple-element.17.refs_0_), channel_id=1, source_target_pairs={{0,3},{1,0},{2,1},{3,2},{4,7},{5,4},{6,5},{7,6},{8,11},{9,8},{10,9... | collective-permute-start | bytes 786440 | tf_op jit(solution)/shard_map/ppermute | solution.py:304
  250.7 3.5 %copy-start.2 = (s16[512,256]{1,0:T(8,128)(2,1)}, s16[512,256]{1,0:T(8,128)(2,1)S(1)}, u32[]{:S(2)}) copy-start(s16[512,256]{1,0:T(8,128)(2,1)S(1)} %collective-permute-done.refs_1_) | copy-start | bytes 786436
  254.2 0.7 copy-start.3
  254.9 0.7 copy-start.4

commit v3 on v2

--- a/solution.py
+++ b/solution.py
@@ -119,6 +119,7 @@
     users, tile = feedback_ref.shape[1:]
     rows = tile // SEGMENTS
     lane = lax.broadcasted_iota(jnp.int32, (users, tile), 1)
+    half_user = user * 0.5
     tiles = []
     for group in range(0, feedback_ref.shape[0], SEGMENTS):
         seen = [feedback_ref[group + p].astype(jnp.float32) for p in range(SEGMENTS)]
@@ -133,12 +134,12 @@
         both = tiles[pair : pair + 2]
         block = jnp.concatenate([arrived_ref[o, at] for _, owners, at in both for o in owners], axis=0)
         scores = lax.dot_general(
-            user, block, (((1,), (1,)), ((), ())), preferred_element_type=jnp.float32
+            half_user, block, (((1,), (1,)), ((), ())), preferred_element_type=jnp.float32
         )
         sides = []
         for h, (mixed, _, _) in enumerate(both):
-            chance = jnp.tanh(scores[:, h * tile : (h + 1) * tile] * 0.5) * 0.5 + 0.5
-            sides.append((chance - mixed).astype(jnp.bfloat16))
+            swing = jnp.tanh(scores[:, h * tile : (h + 1) * tile]) * 0.5
+            sides.append((swing + (0.5 - mixed)).astype(jnp.bfloat16))
         residual = jnp.concatenate(sides, axis=1)
         part = lax.dot_general(
             residual, user, (((0,), (0,)), ((), ())), preferred_element_type=jnp.float32
@@ -164,7 +165,18 @@
     grad_ref[...] += work_on(True, user_ref[...], arrived_ref, feedback_ref, code_ref)
 
 
-def last_kernel(user_ref, arrived_ref, feedback_ref, before_ref, grad_code_ref, code_ref, grad_ref):
+def last_kernel(
+    user_ref,
+    arrived_ref,
+    feedback_ref,
+    before_ref,
+    factors_ref,
+    noise_ref,
+    grad_code_ref,
+    code_ref,
+    base_ref,
+    grad_ref,
+):
     @pl.when(pl.program_id(0) == 0)
     def _():
         grad_ref[...] = before_ref[...]
@@ -174,25 +186,28 @@
     @pl.when(pl.program_id(0) == pl.num_programs(0) - 1)
     def _():
         grad_code_ref[...] = encode(grad_ref[...], USER_RATE)
-
-
-def tiles_of(user_half, arrived, feedback, before=None):
+        factors = factors_ref[...]
+        base_ref[...] = (factors - step_size * prior_weight * factors) + noise_scale * noise_ref[...]
+
+
+def tiles_of(user_half, arrived, feedback, *rest):
     count, rows, rank = arrived.shape
     users, tile = feedback.shape[1:]
-    last = before is not None
-    per_step = 16 if last else 8
+    last = bool(rest)
+    per_step = 16
     return call(
         last_kernel if last else first_kernel,
         (),
-        (user_half, arrived, feedback) + ((before,) if last else ()),
+        (user_half, arrived, feedback, *rest),
         (count // per_step,),
         [whole((users, rank)), along((per_step, rows, rank)), along((per_step, users, tile))]
-        + [whole((users, rank))] * last,
-        [whole((users, rank)), along((per_step, rows, rank))],
+        + [whole((users, rank))] * len(rest),
+        [whole((users, rank)), along((per_step, rows, rank))] + [whole((users, rank))] * last,
         [
             jax.ShapeDtypeStruct((users, rank), jnp.int16 if last else jnp.float32),
             jax.ShapeDtypeStruct((count, rows, rank), jnp.int16),
-        ],
+        ]
+        + [jax.ShapeDtypeStruct((users, rank), jnp.float32)] * last,
         count * rows * users * rank * 6,
         count * users * tile * 2,
         [pltpu.VMEM((users, rank), jnp.float32)] * last,
@@ -245,18 +260,21 @@
     )
 
 
-def last_settle_kernel(z_ref, wanted_ref, code_ref, item_ref, noise_ref, before_ref, out_ref, sum_ref):
+def last_settle_kernel(
+    z_ref, wanted_ref, code_ref, item_ref, noise_ref, before_ref, out_ref, done_ref, sum_ref
+):
     add_codes(wanted_ref, code_ref, sum_ref)
 
     @pl.when(pl.program_id(0) == pl.num_programs(0) - 1)
     def _():
         out_ref[...] = stepped(item_ref[...], sum_ref[...], noise_ref[...])
+        done_ref[...] = jnp.zeros_like(done_ref)
 
 
 def last_settle(z, wanted, codes, item_blocks, noise_blocks, before):
     count, rows, rank = codes.shape
     held = item_blocks.shape[0]
-    per_step = 32
+    per_step = 64
     part = pl.BlockSpec((held, rows, rank), lambda g, z_ref, wanted_ref: (0, z_ref[0], 0))
     return call(
         last_settle_kernel,
@@ -264,8 +282,11 @@
         (codes, item_blocks, noise_blocks, before),
         (count // per_step,),
         [along((per_step, rows, rank)), part, part, ANY],
-        part,
-        jax.ShapeDtypeStruct(item_blocks.shape, jnp.float32),
+        [part, whole((8, 128))],
+        [
+            jax.ShapeDtypeStruct(item_blocks.shape, jnp.float32),
+            jax.ShapeDtypeStruct((8, 128), jnp.float32),
+        ],
         0,
         count * rows * rank * 8,
         [pltpu.VMEM((held, rows, rank), jnp.float32)],
@@ -274,30 +295,38 @@
 
 
 def user_kernel(z_ref, *refs):
-    *code_refs, user_ref, noise_ref, out_ref, grads_ref = refs
-    for j in range(4):
-        grads_ref[(z_ref[0] + 4 - j) % 4] = decode(code_refs[j][...], USER_RATE)
-    total = grads_ref[0] + grads_ref[1] + grads_ref[2] + grads_ref[3]
-    user = user_ref[...]
-    out_ref[...] = (user - step_size * (total + prior_weight * user)) + noise_scale * noise_ref[...]
-
-
-def step_users(z, codes, user_factors, user_noise):
-    users, rank = user_factors.shape
-    steps = 4
+    *code_refs, base_ref, _, out_ref, grads_ref = refs
+    z = z_ref[0]
+    rows = grads_ref.shape[1]
+
+    def piece(i, _):
+        at = row_slice(i, rows)
+        for j in range(4):
+            grads_ref[(z + 4 - j) % 4] = decode(code_refs[j][at, :], USER_RATE)
+        total = grads_ref[0] + grads_ref[1] + grads_ref[2] + grads_ref[3]
+        out_ref[at, :] = base_ref[at, :] - step_size * total
+        return 0
+
+    lax.fori_loop(0, base_ref.shape[0] // rows, piece, 0, unroll=2)
+
+
+def step_users(z, codes, base, after):
+    users, rank = base.shape
+    steps = 2
     share = along((users // steps, rank))
-    return call(
+    return pl.pallas_call(
         user_kernel,
-        (z,),
-        (*codes, user_factors, user_noise),
-        (steps,),
-        [share] * 6,
-        share,
-        jax.ShapeDtypeStruct((users, rank), jnp.float32),
-        0,
-        users * rank * 16,
-        [pltpu.VMEM((4, users // steps, rank), jnp.float32)],
-    )
+        out_shape=jax.ShapeDtypeStruct((users, rank), jnp.float32),
+        grid_spec=pltpu.PrefetchScalarGridSpec(
+            num_scalar_prefetch=1,
+            grid=(steps,),
+            in_specs=[share] * 5 + [whole(after.shape)],
+            out_specs=share,
+            scratch_shapes=[pltpu.VMEM((4, 32, rank), jnp.float32)],
+        ),
+        cost_estimate=pl.CostEstimate(flops=0, bytes_accessed=users * rank * 16, transcendentals=0),
+        compiler_params=pltpu.CompilerParams(vmem_limit_bytes=16 * 1024 * 1024),
+    )(z, *codes, base, after)
 
 
 def shift(array, axis, j):
@@ -323,13 +352,14 @@
     wanted = lax.dynamic_slice_in_dim(picks, own_index, 1, 1)[:, 0]
     grad, codes = tiles_of(user_half, arrived[0], feedback)
     returned = to_all(codes)
-    grad_code, last_codes = tiles_of(user_half, arrived[1], feedback, grad)
+    grad_code, last_codes, base = tiles_of(
+        user_half, arrived[1], feedback, grad, user_factors, user_noise
+    )
     last_returned = to_all(last_codes)
     grad_codes = [shift(grad_code, "z", j) for j in range(4)]
     new_item = first_settle(z, wanted, returned, item_blocks, noise_blocks)
-    new_item = last_settle(z, wanted, last_returned, item_blocks, noise_blocks, new_item)
-    new_item, *grad_codes = lax.optimization_barrier((new_item, *grad_codes))
-    new_user = step_users(z, grad_codes, user_factors, user_noise)
+    new_item, done = last_settle(z, wanted, last_returned, item_blocks, noise_blocks, new_item)
+    new_user = step_users(z, grad_codes, base, done)
     return (new_user, new_item.reshape(item_factors.shape))
 
 

time: 263 us -> 260 us (0.989)
  Pallas kernels: 67.7 us -> 61.5 us
  waiting for transfers between devices: 151 us -> 156 us
    pallas_call x7 -> x6, Pallas kernels: 67.7 us -> 58.8 us  [call(): pl.pallas_call(kernel, out_shape=out_shape, grid_spec=pltpu.PrefetchScala...]
    all_to_all x2, waiting for transfers between devices: 75 us -> 80.1 us  [local(): to_all(pack(first, own, item_pick, item_blocks))]
    pallas_call x0 -> x1, Pallas kernels: none -> 2.73 us  [step_users(): pl.pallas_call(user_kernel, out_shape=jax.ShapeDtypeStruct((users, rank),...]
  transfers between devices with their start and end apart: 7 -> 7, of which waited for: 5 -> 5; matrix products, arithmetic and copies ran while one was open for 1% -> 1% of each run, Pallas kernels for 22% -> 21%
where the time goes in v3:
time: 260 us; the launch traced here: 258 us
  waiting for transfers between devices  156 us (60%)
  Pallas kernels  61.5 us (24%)
  starting transfers between devices  37.1 us (14%)
    all_to_all x2, waiting for transfers between devices, local(): to_all(pack(first, own, item_pick, item_blocks))  80.1 us
    all_to_all x1, waiting for transfers between devices, local(): returned = to_all(codes)  60.6 us
    pallas_call x6, Pallas kernels, call(): pl.pallas_call(kernel, out_shape=out_shape, grid_spec=pltpu.PrefetchScala...  58.8 us
    all_to_all x2, starting transfers between devices, local(): to_all(pack(first, own, item_pick, item_blocks))  17.6 us
    all_to_all x1, waiting for transfers between devices, local(): last_returned = to_all(last_codes)  11.3 us
    all_to_all x1, starting transfers between devices, local(): last_returned = to_all(last_codes)  6.81 us
    all_to_all x1, starting transfers between devices, local(): returned = to_all(codes)  6.55 us
    ppermute x3, starting transfers between devices, shift(): lax.ppermute(array, axis, [(i, (i + j) % 4) for i in range(4)])  6.14 us
  transfers between devices with their start and end apart: 7, of which 5 were waited for; matrix products, arithmetic and copies ran while one was open for 1% of the time, Pallas kernels for 21%

profile of v3, /device:TPU:10, one launch (start us, length us, event | category | flops | bytes accessed | tf_op | source)
XLA Modules:
  0.0 257.7 jit_solution(5424189472072571313)
XLA Ops:
  0.6 5.6 %shard_map.78 = bf16[128,96,256]{2,1,0:T(8,128)(2,1)} custom-call(s32[1]{0:T(128)} %bitcast.1.own_ref, s32[128,128]{1,0:T(8,128)} %pick_ref.3, f32[8,128,256]{2,1,0:T(8,128)} %bitcast.5), custom_call_target="tpu_custom_call" | custom-call | bytes 6291456 | tf_op jit(solution)/shard_map/pallas_call | solution.py:45
  6.3 10.8 %all-to-all-start.1 = ((bf16[128,96,256]{2,1,0:T(8,128)(2,1)}), bf16[128,96,256]{2,1,0:T(8,128)(2,1)}, u32[]{:S(2)}, u32[]{:S(2)}) async-start(bf16[128,96,256]{2,1,0:T(8,128)(2,1)} %shard_map.78), calls=%async_computation.1 | async-start | bytes 12582912 | tf_op jit(solution)/shard_map/all_to_all | solution.py:350
  17.1 0.0 copy-start.3
  17.1 4.5 %shard_map.77 = bf16[128,32,256]{2,1,0:T(8,128)(2,1)} custom-call(s32[1]{0:T(128)} %bitcast.1.own_ref, s32[128,128]{1,0:T(8,128)} %pick_ref.3, f32[8,128,256]{2,1,0:T(8,128)} %bitcast.6), custom_call_target="tpu_custom_call" | custom-call | bytes 2097152 | tf_op jit(solution)/shard_map/pallas_call | solution.py:45
  21.6 71.0 %all-to-all-done.1.arrived_ref = bf16[128,96,256]{2,1,0:T(8,128)(2,1)} async-done(((bf16[128,96,256]{2,1,0:T(8,128)(2,1)}), bf16[128,96,256]{2,1,0:T(8,128)(2,1)}, u32[]{:S(2)}, u32[]{:S(2)}) %all-to-all-start.1) | async-done | bytes 6291488 | tf_op jit(solution)/shard_map/all_to_all | solution.py:350
  92.6 6.8 %all-to-all-start = ((bf16[128,32,256]{2,1,0:T(8,128)(2,1)}), bf16[128,32,256]{2,1,0:T(8,128)(2,1)}, u32[]{:S(2)}, u32[]{:S(2)}) async-start(bf16[128,32,256]{2,1,0:T(8,128)(2,1)} %shard_map.77), calls=%async_computation | async-start | bytes 4194304 | tf_op jit(solution)/shard_map/all_to_all | solution.py:350
  99.4 0.0 copy-done.3
  99.4 0.7 convert_element_type.3.user_ref
  100.2 18.8 %shard_map.79 = (f32[512,256]{1,0:T(8,128)}, s16[128,96,256]{2,1,0:T(8,128)(2,1)}) custom-call(bf16[512,256]{1,0:T(8,128)(2,1)} %convert_element_type.3.user_ref, bf16[128,96,256]{2,1,0:T(8,128)(2,1)} %all-to-all-done.1.arrived_ref, bf16[128,512,128]{2,1,0:T(8,128)(2,1)} %feedback_ref.3), custom_call_target="tpu_custom_call" | custom-call | flops 9663676416 | bytes 16777216 | tf_op jit(solution)/shard_map/pallas_call | solution.py:45
  118.9 9.1 %all-to-all-done.arrived_ref = bf16[128,32,256]{2,1,0:T(8,128)(2,1)} async-done(((bf16[128,32,256]{2,1,0:T(8,128)(2,1)}), bf16[128,32,256]{2,1,0:T(8,128)(2,1)}, u32[]{:S(2)}, u32[]{:S(2)}) %all-to-all-start) | async-done | bytes 2097184 | tf_op jit(solution)/shard_map/all_to_all | solution.py:350
  128.0 6.5 %all-to-all-start.3 = ((s16[128,96,256]{2,1,0:T(8,128)(2,1)}), s16[128,96,256]{2,1,0:T(8,128)(2,1)}, u32[]{:S(2)}, u32[]{:S(2)}) async-start(s16[128,96,256]{2,1,0:T(8,128)(2,1)} %get-tuple-element.15), calls=%async_computation.3 | async-start | bytes 12582912 | tf_op jit(solution)/shard_map/all_to_all | solution.py:354
  134.6 0.0 copy-start.4
  134.6 15.0 %shard_map.80 = (s16[512,256]{1,0:T(8,128)(2,1)}, s16[128,32,256]{2,1,0:T(8,128)(2,1)}, f32[512,256]{1,0:T(8,128)}) custom-call(bf16[512,256]{1,0:T(8,128)(2,1)} %convert_element_type.3.user_ref, bf16[128,32,256]{2,1,0:T(8,128)(2,1)} %all-to-all-done.arrived_ref, bf16[128,512,128]{2,1,0:T(8,128)(2,1)} %feedback_ref.3, ...), custom_call_target="tpu_custom_call" | custom-call | flops 3221225472 | bytes 16777216 | tf_op jit(solution)/shard_map/pallas_call | solution.py:45
  149.6 60.6 %all-to-all-done.3.code_ref = s16[128,96,256]{2,1,0:T(8,128)(2,1)} async-done(((s16[128,96,256]{2,1,0:T(8,128)(2,1)}), s16[128,96,256]{2,1,0:T(8,128)(2,1)}, u32[]{:S(2)}, u32[]{:S(2)}) %all-to-all-start.3) | async-done | bytes 6291488 | tf_op jit(solution)/shard_map/all_to_all | solution.py:354
  210.1 6.8 %all-to-all-start.2 = ((s16[128,32,256]{2,1,0:T(8,128)(2,1)}), s16[128,32,256]{2,1,0:T(8,128)(2,1)}, u32[]{:S(2)}, u32[]{:S(2)}) async-start(s16[128,32,256]{2,1,0:T(8,128)(2,1)} %get-tuple-element.14), calls=%async_computation.2 | async-start | bytes 4194304 | tf_op jit(solution)/shard_map/all_to_all | solution.py:358
  217.0 1.7 collective-permute-start
  218.7 3.2 %collective-permute-start.1 = (s16[512,256]{1,0:T(8,128)(2,1)}, s16[512,256]{1,0:T(8,128)(2,1)}, u32[]{:S(2)}, u32[]{:S(2)}) collective-permute-start(s16[512,256]{1,0:T(8,128)(2,1)} %get-tuple-element.11.refs_0_), channel_id=1, source_target_pairs={{0,2},{1,3},{2,0},{3,1},{4,6},{5,7},{6,4},{7,5},{8,10},{9,11},{10,... | collective-permute-start | bytes 786440 | tf_op jit(solution)/shard_map/ppermute | solution.py:333
  221.9 1.2 collective-permute-start.2
  223.1 0.0 copy-done.4
  223.1 0.8 dynamic-slice_reduce_fusion.wanted_ref
  223.9 0.0 copy-start
  223.9 0.0 copy-start.1
  223.9 10.5 %shard_map.81.before_ref = f32[8,128,256]{2,1,0:T(8,128)} custom-call(s32[1]{0:T(128)} %bitcast.z_ref, s32[128]{0:T(128)} %dynamic-slice_reduce_fusion.wanted_ref, s16[128,96,256]{2,1,0:T(8,128)(2,1)} %all-to-all-done.3.code_ref, f32[8,128,256]{2,1,0:T(8,128)} %bitcast.7, f32[8,128,256]{2,1,0:T(8,128)} %bitcast.9), custom_call_target="tpu_custom_call" | custom-call | bytes 1024 | tf_op jit(solution)/shard_map/pallas_call | solution.py:45
  234.3 11.3 %all-to-all-done.2.code_ref = s16[128,32,256]{2,1,0:T(8,128)(2,1)} async-done(((s16[128,32,256]{2,1,0:T(8,128)(2,1)}), s16[128,32,256]{2,1,0:T(8,128)(2,1)}, u32[]{:S(2)}, u32[]{:S(2)}) %all-to-all-start.2) | async-done | bytes 2097184 | tf_op jit(solution)/shard_map/all_to_all | solution.py:358
  245.6 4.5 %shard_map.82 = (f32[8,128,256]{2,1,0:T(8,128)}, f32[8,128]{1,0:T(8,128)}) custom-call(s32[1]{0:T(128)} %bitcast.z_ref, s32[128]{0:T(128)} %dynamic-slice_reduce_fusion.wanted_ref, s16[128,32,256]{2,1,0:T(8,128)(2,1)} %all-to-all-done.2.code_ref, f32[8,128,256]{2,1,0:T(8,128)} %bitcast.8, f32[8,128,256]{2,1,0:T(8,128)} %bitcast.10, ...), custom_call_target="tpu_custom_call", output_to_operand_aliasing={{0}: (5, {})} | custom-call | bytes 8388608 | tf_op jit(solution)/shard_map/pallas_call | solution.py:45
  250.1 0.0 collective-permute-done.refs_1_
  250.1 4.1 %collective-permute-done.1.refs_2_ = s16[512,256]{1,0:T(8,128)(2,1)} collective-permute-done((s16[512,256]{1,0:T(8,128)(2,1)}, s16[512,256]{1,0:T(8,128)(2,1)}, u32[]{:S(2)}, u32[]{:S(2)}) %collective-permute-start.1) | collective-permute-done | bytes 262176 | tf_op jit(solution)/shard_map/ppermute | solution.py:333
  254.3 0.0 collective-permute-done.2.refs_3_
  254.3 0.0 copy-done
  254.3 0.0 copy-done.1
  254.3 0.0 copy-start.2
  254.3 0.7 copy-done.2
  255.0 2.7 %shard_map.83 = f32[512,256]{1,0:T(8,128)} custom-call(s32[1]{0:T(128)} %bitcast.z_ref, s16[512,256]{1,0:T(8,128)(2,1)S(1)} %copy-done.1, s16[512,256]{1,0:T(8,128)(2,1)} %collective-permute-done.refs_1_, s16[512,256]{1,0:T(8,128)(2,1)} %collective-permute-done.1.refs_2_, s16[512,256]{1,0:T(8,128)(2,1)} %collective-permute-done.2.refs_3_, ...), custom_call_target="tpu_custom_call" | custom-call | bytes 2097152 | tf_op jit(solution)/shard_map/pallas_call | solution.py:317
Async XLA Ops:
  6.3 86.3 %all-to-all-start.1 = ((bf16[128,96,256]{2,1,0:T(8,128)(2,1)}), bf16[128,96,256]{2,1,0:T(8,128)(2,1)}, u32[]{:S(2)}, u32[]{:S(2)}) async-start(bf16[128,96,256]{2,1,0:T(8,128)(2,1)} %shard_map.78), calls=%async_computation.1 | async-start | bytes 12582912 | tf_op jit(solution)/shard_map/all_to_all | solution.py:350
  17.1 82.3 %copy-start.3 = (f32[512,256]{1,0:T(8,128)S(1)}, f32[512,256]{1,0:T(8,128)}, u32[]{:S(2)}) copy-start(f32[512,256]{1,0:T(8,128)} %factors_ref.1) | copy-start | bytes 1572868
  92.6 35.4 %all-to-all-start = ((bf16[128,32,256]{2,1,0:T(8,128)(2,1)}), bf16[128,32,256]{2,1,0:T(8,128)(2,1)}, u32[]{:S(2)}, u32[]{:S(2)}) async-start(bf16[128,32,256]{2,1,0:T(8,128)(2,1)} %shard_map.77), calls=%async_computation | async-start | bytes 4194304 | tf_op jit(solution)/shard_map/all_to_all | solution.py:350
  128.0 82.1 %all-to-all-start.3 = ((s16[128,96,256]{2,1,0:T(8,128)(2,1)}), s16[128,96,256]{2,1,0:T(8,128)(2,1)}, u32[]{:S(2)}, u32[]{:S(2)}) async-start(s16[128,96,256]{2,1,0:T(8,128)(2,1)} %get-tuple-element.15), calls=%async_computation.3 | async-start | bytes 12582912 | tf_op jit(solution)/shard_map/all_to_all | solution.py:354
  134.6 88.5 %copy-start.4 = (s32[128,128]{1,0:T(8,128)S(1)}, s32[128,128]{1,0:T(8,128)}, u32[]{:S(2)}) copy-start(s32[128,128]{1,0:T(8,128)} %pick_ref.3) | copy-start | bytes 196612
  210.1 35.5 %all-to-all-start.2 = ((s16[128,32,256]{2,1,0:T(8,128)(2,1)}), s16[128,32,256]{2,1,0:T(8,128)(2,1)}, u32[]{:S(2)}, u32[]{:S(2)}) async-start(s16[128,32,256]{2,1,0:T(8,128)(2,1)} %get-tuple-element.14), calls=%async_computation.2 | async-start | bytes 4194304 | tf_op jit(solution)/shard_map/all_to_all | solution.py:358
  217.0 33.2 %collective-permute-start = (s16[512,256]{1,0:T(8,128)(2,1)}, s16[512,256]{1,0:T(8,128)(2,1)}, u32[]{:S(2)}, u32[]{:S(2)}) collective-permute-start(s16[512,256]{1,0:T(8,128)(2,1)} %get-tuple-element.11.refs_0_), channel_id=1, source_target_pairs={{0,1},{1,2},{2,3},{3,0},{4,5},{5,6},{6,7},{7,4},{8,9},{9,10},{10,1... | collective-permute-start | bytes 786440 | tf_op jit(solution)/shard_map/ppermute | solution.py:333
  218.7 35.6 %collective-permute-start.1 = (s16[512,256]{1,0:T(8,128)(2,1)}, s16[512,256]{1,0:T(8,128)(2,1)}, u32[]{:S(2)}, u32[]{:S(2)}) collective-permute-start(s16[512,256]{1,0:T(8,128)(2,1)} %get-tuple-element.11.refs_0_), channel_id=1, source_target_pairs={{0,2},{1,3},{2,0},{3,1},{4,6},{5,7},{6,4},{7,5},{8,10},{9,11},{10,... | collective-permute-start | bytes 786440 | tf_op jit(solution)/shard_map/ppermute | solution.py:333
  221.9 32.4 %collective-permute-start.2 = (s16[512,256]{1,0:T(8,128)(2,1)}, s16[512,256]{1,0:T(8,128)(2,1)}, u32[]{:S(2)}, u32[]{:S(2)}) collective-permute-start(s16[512,256]{1,0:T(8,128)(2,1)} %get-tuple-element.11.refs_0_), channel_id=1, source_target_pairs={{0,3},{1,0},{2,1},{3,2},{4,7},{5,4},{6,5},{7,6},{8,11},{9,8},{10,9... | collective-permute-start | bytes 786440 | tf_op jit(solution)/shard_map/ppermute | solution.py:333
  223.9 30.4 %copy-start = (f32[512,256]{1,0:T(8,128)S(1)}, f32[512,256]{1,0:T(8,128)}, u32[]{:S(2)}) copy-start(f32[512,256]{1,0:T(8,128)} %get-tuple-element.12.refs_4_) | copy-start | bytes 1572868
  223.9 30.4 %copy-start.1 = (s16[512,256]{1,0:T(8,128)(2,1)S(1)}, s16[512,256]{1,0:T(8,128)(2,1)}, u32[]{:S(2)}) copy-start(s16[512,256]{1,0:T(8,128)(2,1)} %get-tuple-element.11.refs_0_) | copy-start | bytes 786436
  254.3 0.7 copy-start.2

commit v4 on v3

--- a/solution.py
+++ b/solution.py
@@ -69,11 +69,11 @@
 ANY = pl.BlockSpec(memory_space=pl.ANY)
 
 
-SEGMENTS = 4
+SEGMENTS = 2
 
 
 def segments_of(p, first):
-    return [(p + 1 + k) % SEGMENTS for k in range(SEGMENTS - 1)] if first else [p]
+    return [(p + 1 + k) % SEGMENTS for k in range(SEGMENTS - 1)] if first else [p % SEGMENTS]
 
 
 def row_slice(segment, rows):
@@ -103,10 +103,10 @@
     rows = tile // SEGMENTS * (SEGMENTS - 1 if first else 1)
     return call(
         functools.partial(pack_kernel, first),
-        (own, item_pick),
-        (item_blocks,),
+        (own,),
+        (item_pick, item_blocks),
         (1,),
-        [whole(item_blocks.shape)],
+        [pl.BlockSpec(memory_space=pltpu.SMEM), whole(item_blocks.shape)],
         ANY,
         jax.ShapeDtypeStruct((count, rows, rank), jnp.bfloat16),
         0,
@@ -357,8 +357,8 @@
     )
     last_returned = to_all(last_codes)
     grad_codes = [shift(grad_code, "z", j) for j in range(4)]
-    new_item = first_settle(z, wanted, returned, item_blocks, noise_blocks)
-    new_item, done = last_settle(z, wanted, last_returned, item_blocks, noise_blocks, new_item)
+    new_item = first_settle(z % SEGMENTS, wanted, returned, item_blocks, noise_blocks)
+    new_item, done = last_settle(z % SEGMENTS, wanted, last_returned, item_blocks, noise_blocks, new_item)
     new_user = step_users(z, grad_codes, base, done)
     return (new_user, new_item.reshape(item_factors.shape))
 

time: 260 us -> 253 us (0.973)
  Pallas kernels: 61.5 us -> 58.3 us
    all_to_all x1, waiting for transfers between devices: 60.6 us -> 34.4 us  [local(): returned = to_all(codes)]
    all_to_all x1, waiting for transfers between devices: 11.3 us -> 35.5 us  [local(): last_returned = to_all(last_codes)]
    pallas_call x6, Pallas kernels: 58.8 us -> 55.6 us  [call(): pl.pallas_call(kernel, out_shape=out_shape, grid_spec=pltpu.PrefetchScala...]
where the time goes in v4:
time: 253 us; the launch traced here: 251 us
  waiting for transfers between devices  154 us (61%)
  Pallas kernels  58.3 us (23%)
  starting transfers between devices  35.6 us (14%)
    all_to_all x2, waiting for transfers between devices, local(): to_all(pack(first, own, item_pick, item_blocks))  82.2 us
    pallas_call x6, Pallas kernels, call(): pl.pallas_call(kernel, out_shape=out_shape, grid_spec=pltpu.PrefetchScala...  55.6 us
    all_to_all x1, waiting for transfers between devices, local(): last_returned = to_all(last_codes)  35.5 us
    all_to_all x1, waiting for transfers between devices, local(): returned = to_all(codes)  34.4 us
    all_to_all x2, starting transfers between devices, local(): to_all(pack(first, own, item_pick, item_blocks))  17 us
    all_to_all x1, starting transfers between devices, local(): last_returned = to_all(last_codes)  6.27 us
    ppermute x3, starting transfers between devices, shift(): lax.ppermute(array, axis, [(i, (i + j) % 4) for i in range(4)])  6.21 us
    all_to_all x1, starting transfers between devices, local(): returned = to_all(codes)  6.13 us
  transfers between devices with their start and end apart: 7, of which 5 were waited for; matrix products, arithmetic and copies ran while one was open for 1% of the time, Pallas kernels for 21%

profile of v4, /device:TPU:10, one launch (start us, length us, event | category | flops | bytes accessed | tf_op | source)
XLA Modules:
  0.0 250.5 jit_solution(3517370234753320190)
XLA Ops:
  0.6 3.8 %shard_map.78 = bf16[128,64,256]{2,1,0:T(8,128)(2,1)} custom-call(s32[1]{0:T(128)} %bitcast.1.own_ref, s32[128,128]{1,0:T(8,128)} %pick_ref.3, f32[8,128,256]{2,1,0:T(8,128)} %bitcast.5), custom_call_target="tpu_custom_call" | custom-call | bytes 4194304 | tf_op jit(solution)/shard_map/pallas_call | solution.py:45
  4.4 10.9 %all-to-all-start.1 = ((bf16[128,64,256]{2,1,0:T(8,128)(2,1)}), bf16[128,64,256]{2,1,0:T(8,128)(2,1)}, u32[]{:S(2)}, u32[]{:S(2)}) async-start(bf16[128,64,256]{2,1,0:T(8,128)(2,1)} %shard_map.78), calls=%async_computation.1 | async-start | bytes 8388608 | tf_op jit(solution)/shard_map/all_to_all | solution.py:350
  15.3 3.8 %shard_map.77 = bf16[128,64,256]{2,1,0:T(8,128)(2,1)} custom-call(s32[1]{0:T(128)} %bitcast.1.own_ref, s32[128,128]{1,0:T(8,128)} %pick_ref.3, f32[8,128,256]{2,1,0:T(8,128)} %bitcast.6), custom_call_target="tpu_custom_call" | custom-call | bytes 4194304 | tf_op jit(solution)/shard_map/pallas_call | solution.py:45
  19.1 0.0 copy-start.4
  19.1 47.3 %all-to-all-done.1.arrived_ref = bf16[128,64,256]{2,1,0:T(8,128)(2,1)} async-done(((bf16[128,64,256]{2,1,0:T(8,128)(2,1)}), bf16[128,64,256]{2,1,0:T(8,128)(2,1)}, u32[]{:S(2)}, u32[]{:S(2)}) %all-to-all-start.1) | async-done | bytes 4194336 | tf_op jit(solution)/shard_map/all_to_all | solution.py:350
  66.4 6.1 %all-to-all-start = ((bf16[128,64,256]{2,1,0:T(8,128)(2,1)}), bf16[128,64,256]{2,1,0:T(8,128)(2,1)}, u32[]{:S(2)}, u32[]{:S(2)}) async-start(bf16[128,64,256]{2,1,0:T(8,128)(2,1)} %shard_map.77), calls=%async_computation | async-start | bytes 8388608 | tf_op jit(solution)/shard_map/all_to_all | solution.py:350
  72.6 0.0 copy-done.4
  72.6 0.7 convert_element_type.3.user_ref
  73.3 15.6 %shard_map.79 = (f32[512,256]{1,0:T(8,128)}, s16[128,64,256]{2,1,0:T(8,128)(2,1)}) custom-call(bf16[512,256]{1,0:T(8,128)(2,1)} %convert_element_type.3.user_ref, bf16[128,64,256]{2,1,0:T(8,128)(2,1)} %all-to-all-done.1.arrived_ref, bf16[128,512,128]{2,1,0:T(8,128)(2,1)} %feedback_ref.3), custom_call_target="tpu_custom_call" | custom-call | flops 6442450944 | bytes 16777216 | tf_op jit(solution)/shard_map/pallas_call | solution.py:45
  89.0 34.8 %all-to-all-done.arrived_ref = bf16[128,64,256]{2,1,0:T(8,128)(2,1)} async-done(((bf16[128,64,256]{2,1,0:T(8,128)(2,1)}), bf16[128,64,256]{2,1,0:T(8,128)(2,1)}, u32[]{:S(2)}, u32[]{:S(2)}) %all-to-all-start) | async-done | bytes 4194336 | tf_op jit(solution)/shard_map/all_to_all | solution.py:350
  123.8 6.1 %all-to-all-start.3 = ((s16[128,64,256]{2,1,0:T(8,128)(2,1)}), s16[128,64,256]{2,1,0:T(8,128)(2,1)}, u32[]{:S(2)}, u32[]{:S(2)}) async-start(s16[128,64,256]{2,1,0:T(8,128)(2,1)} %get-tuple-element.15), calls=%async_computation.3 | async-start | bytes 8388608 | tf_op jit(solution)/shard_map/all_to_all | solution.py:354
  129.9 16.8 %shard_map.80 = (s16[512,256]{1,0:T(8,128)(2,1)}, s16[128,64,256]{2,1,0:T(8,128)(2,1)}, f32[512,256]{1,0:T(8,128)}) custom-call(bf16[512,256]{1,0:T(8,128)(2,1)} %convert_element_type.3.user_ref, bf16[128,64,256]{2,1,0:T(8,128)(2,1)} %all-to-all-done.arrived_ref, bf16[128,512,128]{2,1,0:T(8,128)(2,1)} %feedback_ref.3, ...), custom_call_target="tpu_custom_call" | custom-call | flops 6442450944 | bytes 16777216 | tf_op jit(solution)/shard_map/pallas_call | solution.py:45
  146.7 34.4 %all-to-all-done.3.code_ref = s16[128,64,256]{2,1,0:T(8,128)(2,1)} async-done(((s16[128,64,256]{2,1,0:T(8,128)(2,1)}), s16[128,64,256]{2,1,0:T(8,128)(2,1)}, u32[]{:S(2)}, u32[]{:S(2)}) %all-to-all-start.3) | async-done | bytes 4194336 | tf_op jit(solution)/shard_map/all_to_all | solution.py:354
  181.1 0.0 copy-start.1
  181.1 0.0 copy-start.3
  181.1 6.3 %all-to-all-start.2 = ((s16[128,64,256]{2,1,0:T(8,128)(2,1)}), s16[128,64,256]{2,1,0:T(8,128)(2,1)}, u32[]{:S(2)}, u32[]{:S(2)}) async-start(s16[128,64,256]{2,1,0:T(8,128)(2,1)} %get-tuple-element.14), calls=%async_computation.2 | async-start | bytes 8388608 | tf_op jit(solution)/shard_map/all_to_all | solution.py:358
  187.4 0.0 copy-done.1
  187.4 1.8 collective-permute-start
  189.2 3.2 %collective-permute-start.1 = (s16[512,256]{1,0:T(8,128)(2,1)S(1)}, s16[512,256]{1,0:T(8,128)(2,1)}, u32[]{:S(2)}, u32[]{:S(2)}) collective-permute-start(s16[512,256]{1,0:T(8,128)(2,1)S(1)} %copy-done.1), channel_id=1, source_target_pairs={{0,2},{1,3},{2,0},{3,1},{4,6},{5,7},{6,4},{7,5},{8,10},{9,11},{10,... | collective-permute-start | bytes 786440 | tf_op jit(solution)/shard_map/ppermute | solution.py:333
  192.4 1.2 collective-permute-start.2
  193.6 0.0 copy-done.3
  193.6 0.8 dynamic-slice_reduce_fusion.wanted_ref
  194.4 8.9 %shard_map.81.before_ref = f32[8,128,256]{2,1,0:T(8,128)} custom-call(s32[1]{0:T(128)S(6)} %select_n.12.z_ref, s32[128]{0:T(128)} %dynamic-slice_reduce_fusion.wanted_ref, s16[128,64,256]{2,1,0:T(8,128)(2,1)} %all-to-all-done.3.code_ref, f32[8,128,256]{2,1,0:T(8,128)} %bitcast.7, f32[8,128,256]{2,1,0:T(8,128)} %bitcast.9), custom_call_target="tpu_custom_call" | custom-call | bytes 1024 | tf_op jit(solution)/shard_map/pallas_call | solution.py:45
  203.3 0.0 copy-start
  203.3 35.5 %all-to-all-done.2.code_ref = s16[128,64,256]{2,1,0:T(8,128)(2,1)} async-done(((s16[128,64,256]{2,1,0:T(8,128)(2,1)}), s16[128,64,256]{2,1,0:T(8,128)(2,1)}, u32[]{:S(2)}, u32[]{:S(2)}) %all-to-all-start.2) | async-done | bytes 4194336 | tf_op jit(solution)/shard_map/all_to_all | solution.py:358
  238.7 6.8 %shard_map.82 = (f32[8,128,256]{2,1,0:T(8,128)}, f32[8,128]{1,0:T(8,128)}) custom-call(s32[1]{0:T(128)S(6)} %select_n.12.z_ref, s32[128]{0:T(128)} %dynamic-slice_reduce_fusion.wanted_ref, s16[128,64,256]{2,1,0:T(8,128)(2,1)} %all-to-all-done.2.code_ref, f32[8,128,256]{2,1,0:T(8,128)} %bitcast.8, ...), custom_call_target="tpu_custom_call", output_to_operand_aliasing={{0}: (5, {})} | custom-call | bytes 16777216 | tf_op jit(solution)/shard_map/pallas_call | solution.py:45
  245.5 0.0 collective-permute-done.refs_1_
  245.5 1.6 collective-permute-done.1.refs_2_
  247.1 0.0 collective-permute-done.2.refs_3_
  247.1 0.0 copy-done
  247.1 0.0 copy-start.2
  247.1 0.7 copy-done.2
  247.8 2.7 %shard_map.83 = f32[512,256]{1,0:T(8,128)} custom-call(s32[1]{0:T(128)} %bitcast.z_ref, s16[512,256]{1,0:T(8,128)(2,1)S(1)} %copy-done.1, s16[512,256]{1,0:T(8,128)(2,1)} %collective-permute-done.refs_1_, s16[512,256]{1,0:T(8,128)(2,1)} %collective-permute-done.1.refs_2_, s16[512,256]{1,0:T(8,128)(2,1)} %collective-permute-done.2.refs_3_, ...), custom_call_target="tpu_custom_call" | custom-call | bytes 2097152 | tf_op jit(solution)/shard_map/pallas_call | solution.py:317
Async XLA Ops:
  4.4 62.0 %all-to-all-start.1 = ((bf16[128,64,256]{2,1,0:T(8,128)(2,1)}), bf16[128,64,256]{2,1,0:T(8,128)(2,1)}, u32[]{:S(2)}, u32[]{:S(2)}) async-start(bf16[128,64,256]{2,1,0:T(8,128)(2,1)} %shard_map.78), calls=%async_computation.1 | async-start | bytes 8388608 | tf_op jit(solution)/shard_map/all_to_all | solution.py:350
  19.1 53.5 %copy-start.4 = (f32[512,256]{1,0:T(8,128)S(1)}, f32[512,256]{1,0:T(8,128)}, u32[]{:S(2)}) copy-start(f32[512,256]{1,0:T(8,128)} %factors_ref.1) | copy-start | bytes 1572868
  66.4 57.4 %all-to-all-start = ((bf16[128,64,256]{2,1,0:T(8,128)(2,1)}), bf16[128,64,256]{2,1,0:T(8,128)(2,1)}, u32[]{:S(2)}, u32[]{:S(2)}) async-start(bf16[128,64,256]{2,1,0:T(8,128)(2,1)} %shard_map.77), calls=%async_computation | async-start | bytes 8388608 | tf_op jit(solution)/shard_map/all_to_all | solution.py:350
  123.8 57.3 %all-to-all-start.3 = ((s16[128,64,256]{2,1,0:T(8,128)(2,1)}), s16[128,64,256]{2,1,0:T(8,128)(2,1)}, u32[]{:S(2)}, u32[]{:S(2)}) async-start(s16[128,64,256]{2,1,0:T(8,128)(2,1)} %get-tuple-element.15), calls=%async_computation.3 | async-start | bytes 8388608 | tf_op jit(solution)/shard_map/all_to_all | solution.py:354
  181.1 6.3 %copy-start.1 = (s16[512,256]{1,0:T(8,128)(2,1)S(1)}, s16[512,256]{1,0:T(8,128)(2,1)}, u32[]{:S(2)}) copy-start(s16[512,256]{1,0:T(8,128)(2,1)} %get-tuple-element.11.refs_0_) | copy-start | bytes 786436
  181.1 12.5 %copy-start.3 = (s32[128,128]{1,0:T(8,128)S(1)}, s32[128,128]{1,0:T(8,128)}, u32[]{:S(2)}) copy-start(s32[128,128]{1,0:T(8,128)} %pick_ref.3) | copy-start | bytes 196612
  181.1 57.6 %all-to-all-start.2 = ((s16[128,64,256]{2,1,0:T(8,128)(2,1)}), s16[128,64,256]{2,1,0:T(8,128)(2,1)}, u32[]{:S(2)}, u32[]{:S(2)}) async-start(s16[128,64,256]{2,1,0:T(8,128)(2,1)} %get-tuple-element.14), calls=%async_computation.2 | async-start | bytes 8388608 | tf_op jit(solution)/shard_map/all_to_all | solution.py:358
  187.4 58.1 %collective-permute-start = (s16[512,256]{1,0:T(8,128)(2,1)S(1)}, s16[512,256]{1,0:T(8,128)(2,1)}, u32[]{:S(2)}, u32[]{:S(2)}) collective-permute-start(s16[512,256]{1,0:T(8,128)(2,1)S(1)} %copy-done.1), channel_id=1, source_target_pairs={{0,1},{1,2},{2,3},{3,0},{4,5},{5,6},{6,7},{7,4},{8,9},{9,10},{10,1... | collective-permute-start | bytes 786440 | tf_op jit(solution)/shard_map/ppermute | solution.py:333
  189.2 57.9 %collective-permute-start.1 = (s16[512,256]{1,0:T(8,128)(2,1)S(1)}, s16[512,256]{1,0:T(8,128)(2,1)}, u32[]{:S(2)}, u32[]{:S(2)}) collective-permute-start(s16[512,256]{1,0:T(8,128)(2,1)S(1)} %copy-done.1), channel_id=1, source_target_pairs={{0,2},{1,3},{2,0},{3,1},{4,6},{5,7},{6,4},{7,5},{8,10},{9,11},{10,... | collective-permute-start | bytes 786440 | tf_op jit(solution)/shard_map/ppermute | solution.py:333
  192.4 54.7 %collective-permute-start.2 = (s16[512,256]{1,0:T(8,128)(2,1)S(1)}, s16[512,256]{1,0:T(8,128)(2,1)}, u32[]{:S(2)}, u32[]{:S(2)}) collective-permute-start(s16[512,256]{1,0:T(8,128)(2,1)S(1)} %copy-done.1), channel_id=1, source_target_pairs={{0,3},{1,0},{2,1},{3,2},{4,7},{5,4},{6,5},{7,6},{8,11},{9,8},{10,9... | collective-permute-start | bytes 786440 | tf_op jit(solution)/shard_map/ppermute | solution.py:333
  203.3 43.8 %copy-start = (f32[512,256]{1,0:T(8,128)S(1)}, f32[512,256]{1,0:T(8,128)}, u32[]{:S(2)}) copy-start(f32[512,256]{1,0:T(8,128)} %get-tuple-element.12.refs_4_) | copy-start | bytes 1572868
  247.1 0.7 copy-start.2

commit v5 on v4

--- a/solution.py
+++ b/solution.py
@@ -33,7 +33,7 @@
 
 def decode(code, rate):
     code = code.astype(jnp.float32)
-    size = jnp.exp(jnp.abs(code) * (1.0 / rate)) * CODE_FLOOR - CODE_FLOOR
+    size = jnp.exp(jnp.abs(code) * (1.0 / rate)) - 1.0
     return jnp.where(code < 0.0, -size, size)
 
 
@@ -227,7 +227,7 @@
 
 
 def stepped(item, grad, noise):
-    return (item - item_step * (grad + prior_weight * item)) + item_noise_scale * noise
+    return (item - item_step * (grad * CODE_FLOOR + prior_weight * item)) + item_noise_scale * noise
 
 
 def first_settle_kernel(z_ref, wanted_ref, code_ref, item_ref, noise_ref, out_ref, sum_ref):
@@ -244,7 +244,7 @@
 
 def first_settle(z, wanted, codes, item_blocks, noise_blocks):
     count, rows, rank = codes.shape
-    per_step = 16
+    per_step = 32
     block = whole(item_blocks.shape)
     return call(
         first_settle_kernel,
@@ -304,7 +304,7 @@
         for j in range(4):
             grads_ref[(z + 4 - j) % 4] = decode(code_refs[j][at, :], USER_RATE)
         total = grads_ref[0] + grads_ref[1] + grads_ref[2] + grads_ref[3]
-        out_ref[at, :] = base_ref[at, :] - step_size * total
+        out_ref[at, :] = base_ref[at, :] - step_size * CODE_FLOOR * total
         return 0
 
     lax.fori_loop(0, base_ref.shape[0] // rows, piece, 0, unroll=2)
@@ -325,7 +325,7 @@
             scratch_shapes=[pltpu.VMEM((4, 32, rank), jnp.float32)],
         ),
         cost_estimate=pl.CostEstimate(flops=0, bytes_accessed=users * rank * 16, transcendentals=0),
-        compiler_params=pltpu.CompilerParams(vmem_limit_bytes=16 * 1024 * 1024),
+        compiler_params=pltpu.CompilerParams(vmem_limit_bytes=VMEM_LIMIT),
     )(z, *codes, base, after)
 
 

time: 253 us -> 253 us (level)
  transfers between devices with their start and end apart: 7 -> 7, of which waited for: 5 -> 5; matrix products, arithmetic and copies ran while one was open for 1% -> 1% of each run, Pallas kernels for 21% -> 20%
where the time goes in v5:
time: 253 us; the launch traced here: 251 us
  waiting for transfers between devices  156 us (62%)
  Pallas kernels  56.5 us (22%)
  starting transfers between devices  35.6 us (14%)
    all_to_all x2, waiting for transfers between devices, local(): to_all(pack(first, own, item_pick, item_blocks))  82.2 us
    pallas_call x6, Pallas kernels, call(): pl.pallas_call(kernel, out_shape=out_shape, grid_spec=pltpu.PrefetchScala...  53.7 us
    all_to_all x1, waiting for transfers between devices, local(): last_returned = to_all(last_codes)  37.2 us
    all_to_all x1, waiting for transfers between devices, local(): returned = to_all(codes)  34.4 us
    all_to_all x2, starting transfers between devices, local(): to_all(pack(first, own, item_pick, item_blocks))  17 us
    all_to_all x1, starting transfers between devices, local(): last_returned = to_all(last_codes)  6.27 us
    ppermute x3, starting transfers between devices, shift(): lax.ppermute(array, axis, [(i, (i + j) % 4) for i in range(4)])  6.21 us
    all_to_all x1, starting transfers between devices, local(): returned = to_all(codes)  6.13 us
  transfers between devices with their start and end apart: 7, of which 5 were waited for; matrix products, arithmetic and copies ran while one was open for 1% of the time, Pallas kernels for 20%

profile of v5, /device:TPU:10, one launch (start us, length us, event | category | flops | bytes accessed | tf_op | source)
XLA Modules:
  0.0 250.6 jit_solution(17463683029879339250)
XLA Ops:
  0.6 3.8 %shard_map.78 = bf16[128,64,256]{2,1,0:T(8,128)(2,1)} custom-call(s32[1]{0:T(128)} %bitcast.1.own_ref, s32[128,128]{1,0:T(8,128)} %pick_ref.3, f32[8,128,256]{2,1,0:T(8,128)} %bitcast.5), custom_call_target="tpu_custom_call" | custom-call | bytes 4194304 | tf_op jit(solution)/shard_map/pallas_call | solution.py:45
  4.4 10.9 %all-to-all-start.1 = ((bf16[128,64,256]{2,1,0:T(8,128)(2,1)}), bf16[128,64,256]{2,1,0:T(8,128)(2,1)}, u32[]{:S(2)}, u32[]{:S(2)}) async-start(bf16[128,64,256]{2,1,0:T(8,128)(2,1)} %shard_map.78), calls=%async_computation.1 | async-start | bytes 8388608 | tf_op jit(solution)/shard_map/all_to_all | solution.py:350
  15.3 3.8 %shard_map.77 = bf16[128,64,256]{2,1,0:T(8,128)(2,1)} custom-call(s32[1]{0:T(128)} %bitcast.1.own_ref, s32[128,128]{1,0:T(8,128)} %pick_ref.3, f32[8,128,256]{2,1,0:T(8,128)} %bitcast.6), custom_call_target="tpu_custom_call" | custom-call | bytes 4194304 | tf_op jit(solution)/shard_map/pallas_call | solution.py:45
  19.1 0.0 copy-start.1
  19.1 47.3 %all-to-all-done.1.arrived_ref = bf16[128,64,256]{2,1,0:T(8,128)(2,1)} async-done(((bf16[128,64,256]{2,1,0:T(8,128)(2,1)}), bf16[128,64,256]{2,1,0:T(8,128)(2,1)}, u32[]{:S(2)}, u32[]{:S(2)}) %all-to-all-start.1) | async-done | bytes 4194336 | tf_op jit(solution)/shard_map/all_to_all | solution.py:350
  66.4 6.1 %all-to-all-start = ((bf16[128,64,256]{2,1,0:T(8,128)(2,1)}), bf16[128,64,256]{2,1,0:T(8,128)(2,1)}, u32[]{:S(2)}, u32[]{:S(2)}) async-start(bf16[128,64,256]{2,1,0:T(8,128)(2,1)} %shard_map.77), calls=%async_computation | async-start | bytes 8388608 | tf_op jit(solution)/shard_map/all_to_all | solution.py:350
  72.6 0.0 copy-done.1
  72.6 0.7 convert_element_type.3.user_ref
  73.3 15.6 %shard_map.79 = (f32[512,256]{1,0:T(8,128)}, s16[128,64,256]{2,1,0:T(8,128)(2,1)}) custom-call(bf16[512,256]{1,0:T(8,128)(2,1)} %convert_element_type.3.user_ref, bf16[128,64,256]{2,1,0:T(8,128)(2,1)} %all-to-all-done.1.arrived_ref, bf16[128,512,128]{2,1,0:T(8,128)(2,1)} %feedback_ref.3), custom_call_target="tpu_custom_call" | custom-call | flops 6442450944 | bytes 16777216 | tf_op jit(solution)/shard_map/pallas_call | solution.py:45
  89.0 34.8 %all-to-all-done.arrived_ref = bf16[128,64,256]{2,1,0:T(8,128)(2,1)} async-done(((bf16[128,64,256]{2,1,0:T(8,128)(2,1)}), bf16[128,64,256]{2,1,0:T(8,128)(2,1)}, u32[]{:S(2)}, u32[]{:S(2)}) %all-to-all-start) | async-done | bytes 4194336 | tf_op jit(solution)/shard_map/all_to_all | solution.py:350
  123.8 6.1 %all-to-all-start.3 = ((s16[128,64,256]{2,1,0:T(8,128)(2,1)}), s16[128,64,256]{2,1,0:T(8,128)(2,1)}, u32[]{:S(2)}, u32[]{:S(2)}) async-start(s16[128,64,256]{2,1,0:T(8,128)(2,1)} %get-tuple-element.15), calls=%async_computation.3 | async-start | bytes 8388608 | tf_op jit(solution)/shard_map/all_to_all | solution.py:354
  129.9 16.8 %shard_map.80 = (s16[512,256]{1,0:T(8,128)(2,1)}, s16[128,64,256]{2,1,0:T(8,128)(2,1)}, f32[512,256]{1,0:T(8,128)}) custom-call(bf16[512,256]{1,0:T(8,128)(2,1)} %convert_element_type.3.user_ref, bf16[128,64,256]{2,1,0:T(8,128)(2,1)} %all-to-all-done.arrived_ref, bf16[128,512,128]{2,1,0:T(8,128)(2,1)} %feedback_ref.3, ...), custom_call_target="tpu_custom_call" | custom-call | flops 6442450944 | bytes 16777216 | tf_op jit(solution)/shard_map/pallas_call | solution.py:45
  146.7 34.4 %all-to-all-done.3.code_ref = s16[128,64,256]{2,1,0:T(8,128)(2,1)} async-done(((s16[128,64,256]{2,1,0:T(8,128)(2,1)}), s16[128,64,256]{2,1,0:T(8,128)(2,1)}, u32[]{:S(2)}, u32[]{:S(2)}) %all-to-all-start.3) | async-done | bytes 4194336 | tf_op jit(solution)/shard_map/all_to_all | solution.py:354
  181.1 0.0 copy-start.2
  181.1 0.0 copy-start
  181.1 6.3 %all-to-all-start.2 = ((s16[128,64,256]{2,1,0:T(8,128)(2,1)}), s16[128,64,256]{2,1,0:T(8,128)(2,1)}, u32[]{:S(2)}, u32[]{:S(2)}) async-start(s16[128,64,256]{2,1,0:T(8,128)(2,1)} %get-tuple-element.14), calls=%async_computation.2 | async-start | bytes 8388608 | tf_op jit(solution)/shard_map/all_to_all | solution.py:358
  187.4 0.0 copy-done.2
  187.4 1.8 collective-permute-start
  189.2 3.2 %collective-permute-start.1 = (s16[512,256]{1,0:T(8,128)(2,1)S(1)}, s16[512,256]{1,0:T(8,128)(2,1)S(1)}, u32[]{:S(2)}, u32[]{:S(2)}) collective-permute-start(s16[512,256]{1,0:T(8,128)(2,1)S(1)} %copy-done.2), channel_id=1, source_target_pairs={{0,2},{1,3},{2,0},{3,1},{4,6},{5,7},{6,4},{7,5},{8,10},{9,11},{10,... | collective-permute-start | bytes 786440 | tf_op jit(solution)/shard_map/ppermute | solution.py:333
  192.4 1.2 collective-permute-start.2
  193.6 0.0 copy-done
  193.6 0.7 dynamic-slice_reduce_fusion.wanted_ref
  194.3 7.2 %shard_map.81.before_ref = f32[8,128,256]{2,1,0:T(8,128)} custom-call(s32[1]{0:T(128)S(6)} %select_n.12.z_ref, s32[128]{0:T(128)} %dynamic-slice_reduce_fusion.wanted_ref, s16[128,64,256]{2,1,0:T(8,128)(2,1)} %all-to-all-done.3.code_ref, f32[8,128,256]{2,1,0:T(8,128)} %bitcast.7, f32[8,128,256]{2,1,0:T(8,128)} %bitcast.9), custom_call_target="tpu_custom_call" | custom-call | bytes 1024 | tf_op jit(solution)/shard_map/pallas_call | solution.py:45
  201.6 37.2 %all-to-all-done.2.code_ref = s16[128,64,256]{2,1,0:T(8,128)(2,1)} async-done(((s16[128,64,256]{2,1,0:T(8,128)(2,1)}), s16[128,64,256]{2,1,0:T(8,128)(2,1)}, u32[]{:S(2)}, u32[]{:S(2)}) %all-to-all-start.2) | async-done | bytes 4194336 | tf_op jit(solution)/shard_map/all_to_all | solution.py:358
  238.7 6.5 %shard_map.82 = (f32[8,128,256]{2,1,0:T(8,128)}, f32[8,128]{1,0:T(8,128)}) custom-call(s32[1]{0:T(128)S(6)} %select_n.12.z_ref, s32[128]{0:T(128)} %dynamic-slice_reduce_fusion.wanted_ref, s16[128,64,256]{2,1,0:T(8,128)(2,1)} %all-to-all-done.2.code_ref, f32[8,128,256]{2,1,0:T(8,128)} %bitcast.8, ...), custom_call_target="tpu_custom_call", output_to_operand_aliasing={{0}: (5, {})} | custom-call | bytes 16777216 | tf_op jit(solution)/shard_map/pallas_call | solution.py:45
  245.2 0.0 collective-permute-done.refs_1_
  245.2 0.0 copy-start.3
  245.2 1.8 collective-permute-done.1.refs_2_
  247.0 0.0 copy-start.4
  247.0 0.0 collective-permute-done.2.refs_3_
  247.0 0.0 copy-done.3
  247.0 0.7 copy-done.4
  247.7 2.9 %shard_map.83 = f32[512,256]{1,0:T(8,128)} custom-call(s32[1]{0:T(128)} %bitcast.z_ref, s16[512,256]{1,0:T(8,128)(2,1)} %get-tuple-element.11.refs_0_, s16[512,256]{1,0:T(8,128)(2,1)} %copy-done.3, s16[512,256]{1,0:T(8,128)(2,1)} %copy-done.4, s16[512,256]{1,0:T(8,128)(2,1)} %collective-permute-done.2.refs_3_, f32[512,256]{1,0:T(8,128)} %get-tuple-element.12.refs_4_, ...), custom_call_target="tpu_custom_call" | custom-call | bytes 2097152 | tf_op jit(solution)/shard_map/pallas_call | solution.py:317
Async XLA Ops:
  4.4 62.0 %all-to-all-start.1 = ((bf16[128,64,256]{2,1,0:T(8,128)(2,1)}), bf16[128,64,256]{2,1,0:T(8,128)(2,1)}, u32[]{:S(2)}, u32[]{:S(2)}) async-start(bf16[128,64,256]{2,1,0:T(8,128)(2,1)} %shard_map.78), calls=%async_computation.1 | async-start | bytes 8388608 | tf_op jit(solution)/shard_map/all_to_all | solution.py:350
  19.1 53.5 %copy-start.1 = (f32[512,256]{1,0:T(8,128)S(1)}, f32[512,256]{1,0:T(8,128)}, u32[]{:S(2)}) copy-start(f32[512,256]{1,0:T(8,128)} %factors_ref.1) | copy-start | bytes 1572868
  66.4 57.4 %all-to-all-start = ((bf16[128,64,256]{2,1,0:T(8,128)(2,1)}), bf16[128,64,256]{2,1,0:T(8,128)(2,1)}, u32[]{:S(2)}, u32[]{:S(2)}) async-start(bf16[128,64,256]{2,1,0:T(8,128)(2,1)} %shard_map.77), calls=%async_computation | async-start | bytes 8388608 | tf_op jit(solution)/shard_map/all_to_all | solution.py:350
  123.8 57.3 %all-to-all-start.3 = ((s16[128,64,256]{2,1,0:T(8,128)(2,1)}), s16[128,64,256]{2,1,0:T(8,128)(2,1)}, u32[]{:S(2)}, u32[]{:S(2)}) async-start(s16[128,64,256]{2,1,0:T(8,128)(2,1)} %get-tuple-element.15), calls=%async_computation.3 | async-start | bytes 8388608 | tf_op jit(solution)/shard_map/all_to_all | solution.py:354
  181.1 6.3 %copy-start.2 = (s16[512,256]{1,0:T(8,128)(2,1)S(1)}, s16[512,256]{1,0:T(8,128)(2,1)}, u32[]{:S(2)}) copy-start(s16[512,256]{1,0:T(8,128)(2,1)} %get-tuple-element.11.refs_0_) | copy-start | bytes 786436
  181.1 12.5 %copy-start = (s32[128,128]{1,0:T(8,128)S(1)}, s32[128,128]{1,0:T(8,128)}, u32[]{:S(2)}) copy-start(s32[128,128]{1,0:T(8,128)} %pick_ref.3) | copy-start | bytes 196612
  181.1 57.6 %all-to-all-start.2 = ((s16[128,64,256]{2,1,0:T(8,128)(2,1)}), s16[128,64,256]{2,1,0:T(8,128)(2,1)}, u32[]{:S(2)}, u32[]{:S(2)}) async-start(s16[128,64,256]{2,1,0:T(8,128)(2,1)} %get-tuple-element.14), calls=%async_computation.2 | async-start | bytes 8388608 | tf_op jit(solution)/shard_map/all_to_all | solution.py:358
  187.4 57.8 %collective-permute-start = (s16[512,256]{1,0:T(8,128)(2,1)S(1)}, s16[512,256]{1,0:T(8,128)(2,1)S(1)}, u32[]{:S(2)}, u32[]{:S(2)}) collective-permute-start(s16[512,256]{1,0:T(8,128)(2,1)S(1)} %copy-done.2), channel_id=1, source_target_pairs={{0,1},{1,2},{2,3},{3,0},{4,5},{5,6},{6,7},{7,4},{8,9},{9,10},{10,1... | collective-permute-start | bytes 786440 | tf_op jit(solution)/shard_map/ppermute | solution.py:333
  189.2 57.8 %collective-permute-start.1 = (s16[512,256]{1,0:T(8,128)(2,1)S(1)}, s16[512,256]{1,0:T(8,128)(2,1)S(1)}, u32[]{:S(2)}, u32[]{:S(2)}) collective-permute-start(s16[512,256]{1,0:T(8,128)(2,1)S(1)} %copy-done.2), channel_id=1, source_target_pairs={{0,2},{1,3},{2,0},{3,1},{4,6},{5,7},{6,4},{7,5},{8,10},{9,11},{10,... | collective-permute-start | bytes 786440 | tf_op jit(solution)/shard_map/ppermute | solution.py:333
  192.4 54.6 %collective-permute-start.2 = (s16[512,256]{1,0:T(8,128)(2,1)S(1)}, s16[512,256]{1,0:T(8,128)(2,1)}, u32[]{:S(2)}, u32[]{:S(2)}) collective-permute-start(s16[512,256]{1,0:T(8,128)(2,1)S(1)} %copy-done.2), channel_id=1, source_target_pairs={{0,3},{1,0},{2,1},{3,2},{4,7},{5,4},{6,5},{7,6},{8,11},{9,8},{10,9... | collective-permute-start | bytes 786440 | tf_op jit(solution)/shard_map/ppermute | solution.py:333
  245.2 1.8 copy-start.3
  247.0 0.7 copy-start.4
